TPU v7x, 256 devices: a whole 4x4x8 slice. The times are simulated.
256 devices in a mesh: member: 4 (over x), grid: 64 (over y, z, core).
Axes of the slice: x: 4, y: 4, z: 8, core: 2. Of those that a mesh axis runs over, the one named last changes fastest.
Arguments:
- states: bfloat16 [16, 2048, 1024], P('member', 'grid')
- ln_gain: float32 [1024], replicated, may hold values from 0.1 to 1.9
- w_qkv: bfloat16 [1024, 3072], replicated
- w_out: bfloat16 [1024, 1024], replicated, may hold values from -0.75 to 0.75
- w_head: bfloat16 [1024, 100], replicated, may hold values from -0.1875 to 0.1875
- targets: float32 [2048, 100], P('grid'), may hold values from -6 to 6
- neighbours: int32 [128, 4], P('grid'), may hold values from 0 to 127, as said below
- counts: int32 [64], P('grid'), may hold values from 16 to 32
Outputs:
- loss: float32 [], replicated
- grad_states: bfloat16 [16, 2048, 1024], P('member', 'grid')
- head_grad: float32 [1024, 100], replicated
Inputs may be any that keep to these rules, and one draw needn't show every extreme that they name: neighbours[t, 0] is t; the other entries of row t are distinct tiles within 2 of t, except near the first and last tiles, where an entry beyond the grid is reflected to the other side of t and may then repeat.
All inputs are finite; a program needn't handle non-finite values.
Results may differ from a plain program's by a relative error of at most 0.02.
The roundings to bfloat16 on the way count: a program that leaves them out, or rounds other values in their place, can miss the bound.
Values may be sent and summed in bfloat16 or wider, within the bound.
A program may use at most 128 MiB of HBM per device.

v0:
```python
import functools

import jax
import jax.numpy as jnp
from jax import lax
from jax.experimental import pallas as pl
from jax.experimental.pallas import tpu as pltpu
from jax.sharding import PartitionSpec as P

HEADS = 16
VARS = 100
TILE = 16
EPS = 1e-05
DELTA = 0.1
LANES = 128
PACK = 4
INNER = 16
BLOCK = 256
MESH = pl.DeviceIdType.MESH
F32 = jnp.float32
BF16 = jnp.bfloat16

NN = (((1,), (0,)), ((), ()))
NT = (((1,), (1,)), ((), ()))
TN = (((0,), (0,)), ((), ()))


def dot(a, b, dims):
    return lax.dot_general(a, b, dims, preferred_element_type=F32)


def kernel(
    sizes,
    states,
    gain,
    wqkv_hbm,
    wout_hbm,
    whead,
    targets,
    neighbours,
    counts,
    loss,
    grad,
    head_out,
    wqkv,
    wout,
    wpad,
    tpad,
    hall,
    query,
    kv,
    normed,
    inverse,
    cnt,
    hmask,
    probs,
    attn,
    mixed,
    ens,
    gradb,
    local,
    part,
    plane,
    full,
    dmixed,
    dmixedb,
    dattn,
    dquery,
    dkv,
    dsend,
    drecv,
    dhid,
    wsem,
    halo_s,
    halo_r,
    pred_s,
    pred_r,
    part_s,
    part_r,
    plane_s,
    plane_r,
    full_s,
    full_r,
    back_s,
    back_r,
):
    n_member, n_grid, n_inner = sizes
    n_outer = n_grid // n_inner
    group = n_member * n_outer
    members, points, width = states.shape
    window = hall.shape[1]
    flat = members * points
    cols = PACK * (width // HEADS)
    chunks = width // BLOCK
    packs = HEADS // PACK
    total_members = members * n_member
    piece = width // group

    me_m = lax.axis_index("member")
    me_g = lax.axis_index("grid")
    outer = me_g // n_inner
    inner = lax.rem(me_g, n_inner)
    up = lax.rem(me_g + 1, n_grid)
    down = lax.rem(me_g + n_grid - 1, n_grid)
    mine = me_m * n_outer + outer

    def group_peer(k):
        m = lax.rem(me_m + k // n_outer, n_member)
        o = lax.rem(outer + lax.rem(k, n_outer), n_outer)
        return m, o

    def inner_peer(k):
        return (me_m, outer * n_inner + lax.rem(inner + k, n_inner))

    barrier = pltpu.get_barrier_semaphore()

    def greet_group(k, c):
        m, o = group_peer(k)
        pl.semaphore_signal(barrier, inc=1, device_id=(m, o * n_inner + inner), device_id_type=MESH)
        return c

    def greet_inner(k, c):
        pl.semaphore_signal(barrier, inc=1, device_id=inner_peer(k), device_id_type=MESH)
        return c

    for side in (up, down):
        pl.semaphore_signal(barrier, inc=1, device_id=(me_m, side), device_id_type=MESH)
    lax.fori_loop(1, group, greet_group, 0)
    lax.fori_loop(1, n_inner, greet_inner, 0)

    wide = 2 * BLOCK
    n_wide = 3 * width // wide
    weight_copies = [
        pltpu.make_async_copy(
            wqkv_hbm.at[:, pl.ds(c * wide, wide)], wqkv.at[:, pl.ds(c * wide, wide)], wsem.at[c]
        )
        for c in range(n_wide)
    ]
    weight_copies.append(pltpu.make_async_copy(wout_hbm, wout, wsem.at[n_wide]))
    for copy in weight_copies:
        copy.start()

    for m in range(members):
        values = states[m].astype(F32)
        centre = jnp.mean(values, axis=-1, keepdims=True)
        centred = values - centre
        spread = jnp.mean(centred * centred, axis=-1, keepdims=True)
        inv = lax.rsqrt(spread + EPS)
        norm = centred * inv
        normed[m] = norm
        inverse[m] = inv
        hall[m, pl.ds(points, points), :] = (norm * gain[...]).astype(BF16)

    pl.semaphore_wait(barrier, 2 + (group - 1) + (n_inner - 1))

    own_rows = hall.at[:, pl.ds(points, points), :]
    halo = [
        pltpu.make_async_remote_copy(
            src_ref=own_rows,
            dst_ref=hall.at[:, pl.ds(start, points), :],
            send_sem=halo_s.at[i],
            recv_sem=halo_r.at[i],
            device_id=(me_m, side),
            device_id_type=MESH,
        )
        for i, (start, side) in enumerate(((0, up), (2 * points, down)))
    ]
    for copy in halo:
        copy.start()

    key_tile = 2 * me_g - 2 + lax.broadcasted_iota(jnp.int32, (window, LANES), 0) // TILE
    lane = lax.broadcasted_iota(jnp.int32, (window, LANES), 1)
    query_tile = lax.rem(lane, points) // TILE
    number = jnp.zeros((window, LANES), F32)
    for t in range(points // TILE):
        for e in range(neighbours.shape[1]):
            hit = (key_tile == neighbours[t, e]) & (query_tile == t)
            number = number + jnp.where(hit, 1.0, 0.0)
    cnt[...] = number
    rows_i = lax.broadcasted_iota(jnp.int32, (PACK * points, cols), 0) // points
    cols_i = lax.broadcasted_iota(jnp.int32, (PACK * points, cols), 1) // (cols // PACK)
    hmask[...] = jnp.where(rows_i == cols_i, 1.0, 0.0)
    wpad[...] = jnp.zeros_like(wpad)
    wpad[:, pl.ds(0, VARS)] = whead[...]
    tpad[...] = jnp.zeros_like(tpad)
    tpad[:, pl.ds(0, VARS)] = targets[...]

    own = hall[:, pl.ds(points, points), :].reshape(flat, width)
    for c in range(width // wide):
        weight_copies[c].wait()
        q = dot(own, wqkv[:, pl.ds(c * wide, wide)], NN).astype(BF16)
        query[:, pl.ds(c * wide, wide)] = q * jnp.asarray((width // HEADS) ** -0.5, BF16)

    for c in range(width // wide, n_wide):
        weight_copies[c].wait()
    weight_copies[n_wide].wait()
    for copy in halo:
        copy.wait_recv()

    def keys_values(c, carry):
        here = pl.ds(pl.multiple_of(c * BLOCK, BLOCK), BLOCK)
        there = pl.ds(pl.multiple_of(width + c * BLOCK, BLOCK), BLOCK)
        rows = hall[...].reshape(members * window, width)
        kv[:, here] = dot(rows, wqkv[:, there], NN).astype(BF16)
        return carry

    lax.fori_loop(0, 2 * width // BLOCK, keys_values, 0)

    def spread_heads(rows):
        return jnp.concatenate([rows] * PACK, axis=0) * hmask[...].astype(BF16)

    def pick_heads(rows):
        rows = rows * hmask[...]
        return jnp.sum(rows.reshape(PACK, points, cols), axis=0)

    def forward(m, carry):
        rows = pl.ds(pl.multiple_of(m * points, points), points)
        keys = pl.ds(pl.multiple_of(m * window, TILE), window)
        number = cnt[...]
        for h in range(packs):
            here = pl.ds(h * cols, cols)
            there = pl.ds(width + h * cols, cols)
            scores = dot(kv[keys, here], spread_heads(query[rows, here]), NT)
            scores = jnp.where(number > 0.0, scores, -3e38)
            top = jnp.max(scores, axis=0, keepdims=True)
            expo = jnp.exp(scores - top)
            prob = expo / jnp.sum(number * expo, axis=0, keepdims=True)
            probs[m, h] = prob
            weight = (number * prob.astype(BF16).astype(F32)).astype(BF16)
            attn[rows, here] = pick_heads(dot(weight, kv[keys, there], TN)).astype(BF16)
        return carry

    lax.fori_loop(0, members, forward, 0)

    flat_states = states[...].reshape(flat, width)
    for c in range(chunks):
        here = pl.ds(c * BLOCK, BLOCK)
        proj = dot(attn[...], wout[:, here], NN)
        mixed[:, here] = (flat_states[:, c * BLOCK : (c + 1) * BLOCK].astype(F32) + proj).astype(BF16)
    ens[0] = dot(mixed[...], wpad[...], NN).astype(BF16)

    def pred_copy(k):
        return pltpu.make_async_remote_copy(
            src_ref=ens.at[0],
            dst_ref=ens.at[k],
            send_sem=pred_s.at[k],
            recv_sem=pred_r.at[k],
            device_id=(lax.rem(me_m + k, n_member), me_g),
            device_id_type=MESH,
        )

    for k in range(1, n_member):
        pred_copy(k).start()
    for k in range(1, n_member):
        pred_copy(k).wait_recv()

    row = lax.broadcasted_iota(jnp.int32, (points, LANES), 0)
    column = lax.broadcasted_iota(jnp.int32, (points, LANES), 1)
    valid = (row < counts[0]) & (column < VARS)

    def crps(i, total):
        rows = pl.ds(pl.multiple_of(i * points, points), points)
        one = ens[0, rows, :].astype(F32)
        pull = jnp.zeros((points, LANES), F32)
        apart = jnp.zeros((points, LANES), F32)
        for k in range(n_member):
            for j in range(members):
                gap = one - ens[k, pl.ds(j * points, points), :].astype(F32)
                square = gap * gap + DELTA * DELTA
                root = lax.rsqrt(square)
                pull = pull + gap * root
                apart = apart + square * root
        miss = one - tpad[...]
        square = miss * miss + DELTA * DELTA
        root = lax.rsqrt(square)
        slope = miss * root - pull * (1.0 / (total_members - 1))
        gradb[rows, :] = jnp.where(valid, slope, 0.0).astype(BF16)
        term = square * root - (apart - DELTA) * (0.5 / (total_members - 1))
        return total + jnp.where(valid, term, 0.0)

    terms = lax.fori_loop(0, members, crps, jnp.zeros((points, LANES), F32))
    loss_part = jnp.sum(jnp.sum(terms, axis=1, keepdims=True), axis=0, keepdims=True)

    def with_loss(value):
        spot = lax.broadcasted_iota(jnp.int32, (1, LANES), 1)
        high = value.astype(BF16).astype(F32)
        return jnp.where(spot == VARS, high, jnp.where(spot == VARS + 1, value - high, 0.0))

    def loss_of(rows):
        spot = lax.broadcasted_iota(jnp.int32, (1, LANES), 1)
        kept = jnp.where((spot == VARS) | (spot == VARS + 1), rows[0:1, :], 0.0)
        return jnp.sum(kept, axis=1, keepdims=True)

    tail = with_loss(loss_part)
    per = BLOCK // piece
    for c in range(chunks):
        here = pl.ds(c * BLOCK, BLOCK)
        part_sum = dot(mixed[:, here], gradb[...], TN) + tail
        if piece <= BLOCK:
            local[pl.ds(c * per, per)] = part_sum.reshape(per, piece, LANES).astype(BF16)

    def part_copy(k):
        m, o = group_peer(k)
        return pltpu.make_async_remote_copy(
            src_ref=local.at[m * n_outer + o],
            dst_ref=part.at[k],
            send_sem=part_s.at[k],
            recv_sem=part_r.at[k],
            device_id=(m, o * n_inner + inner),
            device_id_type=MESH,
        )

    def plane_copy(k):
        return pltpu.make_async_remote_copy(
            src_ref=plane.at[inner],
            dst_ref=plane.at[inner],
            send_sem=plane_s.at[k],
            recv_sem=plane_r.at[k],
            device_id=inner_peer(k),
            device_id_type=MESH,
        )

    def full_copy(k):
        m, o = group_peer(k)
        return pltpu.make_async_remote_copy(
            src_ref=full.at[mine],
            dst_ref=full.at[mine],
            send_sem=full_s.at[k],
            recv_sem=full_r.at[k],
            device_id=(m, o * n_inner + inner),
            device_id_type=MESH,
        )

    def each(count, make, act):
        def step(k, c):
            getattr(make(k), act)()
            return c

        lax.fori_loop(1, count, step, 0)

    each(group, part_copy, "start")

    for c in range(chunks):
        here = pl.ds(c * BLOCK, BLOCK)
        step = dot(gradb[...], wpad[here, :], NT)
        dmixed[:, here] = step
        dmixedb[:, here] = step.astype(BF16)
    for c in range(chunks):
        here = pl.ds(c * BLOCK, BLOCK)
        dattn[:, here] = dot(dmixedb[...], wout[here, :], NT).astype(BF16)

    scale = (width // HEADS) ** -0.5

    def backward(m, carry):
        rows = pl.ds(pl.multiple_of(m * points, points), points)
        keys = pl.ds(pl.multiple_of(m * window, TILE), window)
        number = cnt[...]
        for h in range(packs):
            here = pl.ds(h * cols, cols)
            there = pl.ds(width + h * cols, cols)
            out = spread_heads(dattn[rows, here])
            prob = probs[m, h]
            dprob = dot(kv[keys, there], out, NT)
            lean = jnp.sum(number * dprob * prob, axis=0, keepdims=True)
            dscore = (prob * (dprob - lean)).astype(BF16)
            dscore = (number * dscore.astype(F32)).astype(BF16)
            weight = (number * prob.astype(BF16).astype(F32)).astype(BF16)
            dquery[rows, here] = (pick_heads(dot(dscore, kv[keys, here], TN)) * scale).astype(BF16)
            dkv[keys, here] = dot(dscore, spread_heads(query[rows, here]), NN).astype(BF16)
            dkv[keys, there] = dot(weight, out, NN).astype(BF16)
        return carry

    lax.fori_loop(0, members, backward, 0)

    each(group, part_copy, "wait_recv")
    piece_sum = local[mine].astype(F32)
    for k in range(1, group):
        piece_sum = piece_sum + part[k].astype(F32)
    spare = lax.broadcasted_iota(jnp.int32, (1, LANES), 1) >= VARS
    plane[inner] = jnp.where(spare, with_loss(loss_of(piece_sum)), piece_sum).astype(BF16)
    each(n_inner, plane_copy, "start")

    def back_copy(side, c):
        return pltpu.make_async_remote_copy(
            src_ref=dsend.at[side, c],
            dst_ref=drecv.at[side, c],
            send_sem=back_s.at[side, c],
            recv_sem=back_r.at[side, c],
            device_id=(me_m, down if side == 0 else up),
            device_id_type=MESH,
        )

    for c in range(chunks):
        here = pl.ds(c * BLOCK, BLOCK)
        step = dot(dkv[...], wqkv[here, pl.ds(width, 2 * width)], NT)
        step = step.reshape(members, window, BLOCK)
        for side, start in ((0, 0), (1, 2 * points)):
            dsend[side, c] = step[:, start : start + points].astype(BF16)
            back_copy(side, c).start()
        dhid[:, :, here] = step[:, points : 2 * points]

    each(n_inner, plane_copy, "wait_recv")
    plane_sum = plane[0].astype(F32)
    for k in range(1, n_inner):
        plane_sum = plane_sum + plane[k].astype(F32)
    plane_loss = loss_of(plane_sum)
    plane_sum = plane_sum * (1.0 / (points * n_grid))
    full[mine] = plane_sum.astype(BF16)
    loss[...] = plane_loss * (1.0 / (points * n_grid * VARS * total_members))
    each(group, full_copy, "start")

    for c in range(chunks):
        here = pl.ds(c * BLOCK, BLOCK)
        step = dot(dquery[...], wqkv[here, pl.ds(0, width)], NT)
        dhid[:, :, here] = dhid[:, :, here] + step.reshape(members, points, BLOCK)

    for c in range(chunks):
        here = pl.ds(c * BLOCK, BLOCK)
        for side in range(2):
            back_copy(side, c).wait_recv()
        extra = drecv[0, c].astype(F32) + drecv[1, c].astype(F32)
        dhid[:, :, here] = dhid[:, :, here] + extra

    for m in range(members):
        dnormed = dhid[m] * gain[...]
        norm = normed[m]
        first = jnp.mean(dnormed, axis=-1, keepdims=True)
        second = jnp.mean(dnormed * norm, axis=-1, keepdims=True)
        dstates = inverse[m] * (dnormed - first - norm * second)
        grad[m] = (dstates + dmixed[pl.ds(m * points, points), :]).astype(BF16)

    each(group, full_copy, "wait_recv")
    for k in range(group):
        head_out[pl.ds(k * piece, piece), :] = full[k][:, :VARS].astype(F32)

    for copy in halo:
        copy.wait_send()
    for k in range(1, n_member):
        pred_copy(k).wait_send()
    each(group, part_copy, "wait_send")
    each(n_inner, plane_copy, "wait_send")
    each(group, full_copy, "wait_send")
    for c in range(chunks):
        for side in range(2):
            back_copy(side, c).wait_send()


def body(sizes, states, ln_gain, w_qkv, w_out, w_head, targets, neighbours, counts):
    n_member, n_grid, n_inner = sizes
    members, points, width = states.shape
    flat = members * points
    window = 3 * points
    group = n_member * (n_grid // n_inner)
    chunks = width // BLOCK
    piece = width // group
    cols = PACK * (width // HEADS)
    vmem = pl.BlockSpec(memory_space=pltpu.VMEM)
    smem = pl.BlockSpec(memory_space=pltpu.SMEM)
    hbm = pl.BlockSpec(memory_space=pl.ANY)
    dma = pltpu.SemaphoreType.DMA
    loss, grad, head = pl.pallas_call(
        functools.partial(kernel, sizes),
        out_shape=(
            jax.ShapeDtypeStruct((1, 1), F32),
            jax.ShapeDtypeStruct((members, points, width), BF16),
            jax.ShapeDtypeStruct((width, VARS), F32),
        ),
        in_specs=[vmem, vmem, hbm, hbm, vmem, vmem, smem, smem],
        out_specs=(vmem, vmem, vmem),
        scratch_shapes=[
            pltpu.VMEM((width, 3 * width), BF16),
            pltpu.VMEM((width, width), BF16),
            pltpu.VMEM((width, LANES), BF16),
            pltpu.VMEM((points, LANES), F32),
            pltpu.VMEM((members, window, width), BF16),
            pltpu.VMEM((flat, width), BF16),
            pltpu.VMEM((members * window, 2 * width), BF16),
            pltpu.VMEM((members, points, width), F32),
            pltpu.VMEM((members, points, 1), F32),
            pltpu.VMEM((window, LANES), F32),
            pltpu.VMEM((PACK * points, cols), F32),
            pltpu.VMEM((members, HEADS // PACK, window, PACK * points), F32),
            pltpu.VMEM((flat, width), BF16),
            pltpu.VMEM((flat, width), BF16),
            pltpu.VMEM((n_member, flat, LANES), BF16),
            pltpu.VMEM((flat, LANES), BF16),
            pltpu.VMEM((group, piece, LANES), BF16),
            pltpu.VMEM((group, piece, LANES), BF16),
            pltpu.VMEM((n_inner, piece, LANES), BF16),
            pltpu.VMEM((group, piece, LANES), BF16),
            pltpu.VMEM((flat, width), F32),
            pltpu.VMEM((flat, width), BF16),
            pltpu.VMEM((flat, width), BF16),
            pltpu.VMEM((flat, width), BF16),
            pltpu.VMEM((members * window, 2 * width), BF16),
            pltpu.VMEM((2, chunks, members, points, BLOCK), BF16),
            pltpu.VMEM((2, chunks, members, points, BLOCK), BF16),
            pltpu.VMEM((members, points, width), F32),
            dma((3 * width // (2 * BLOCK) + 1,)),
            dma((2,)),
            dma((2,)),
            dma((n_member,)),
            dma((n_member,)),
            dma((group,)),
            dma((group,)),
            dma((n_inner,)),
            dma((n_inner,)),
            dma((group,)),
            dma((group,)),
            dma((2, chunks)),
            dma((2, chunks)),
        ],
        compiler_params=pltpu.CompilerParams(
            collective_id=0, has_side_effects=True, vmem_limit_bytes=48 * 1024 * 1024
        ),
    )(states, ln_gain.reshape(1, width), w_qkv, w_out, w_head, targets, neighbours, counts)
    return (loss.reshape(()), grad, head)


def solution(mesh):
    placed = (
        P("member", "grid", None),
        P(),
        P(),
        P(),
        P(),
        P("grid", None),
        P("grid", None),
        P("grid"),
    )
    n_member, n_grid = mesh.shape["member"], mesh.shape["grid"]
    sizes = (n_member, n_grid, min(INNER, n_grid // 2))
    return jax.shard_map(
        functools.partial(body, sizes),
        mesh=mesh,
        in_specs=placed,
        out_specs=(P(), P("member", "grid", None), P()),
        check_vma=False,
    )
```

profile of v0, /device:TPU:1, one launch (start us, length us, event | category | flops | bytes accessed | tf_op | source)
XLA Modules:
  0.0 63.0 jit_solution(13711136413887854330)
XLA Ops:
  1.3 1.1 %copy.11.whead = bf16[1024,100]{1,0:T(8,128)(2,1)S(1)} copy(bf16[1024,100]{0,1:T(8,128)(2,1)} %param.12) | data formatting | bytes 409600 | tf_op args[4]
  2.4 0.0 copy-start
  2.4 1.6 %copy-done = bf16[1024,1024]{1,0:T(8,128)(2,1)S(1)} copy-done((bf16[1024,1024]{1,0:T(8,128)(2,1)S(1)}, bf16[1024,1024]{1,0:T(8,128)(2,1)}, u32[]{:S(2)}) %copy-start) | copy-done | bytes 2097176
  4.0 0.0 copy-start.1
  4.0 0.9 %copy-done.1 = bf16[4,32,1024]{2,1,0:T(8,128)(2,1)S(1)} copy-done((bf16[4,32,1024]{2,1,0:T(8,128)(2,1)S(1)}, bf16[4,32,1024]{2,1,0:T(8,128)(2,1)}, u32[]{:S(2)}) %copy-start.1) | copy-done | bytes 262168
  4.9 0.0 copy-start.2
  4.9 0.7 %copy-done.2 = f32[32,100]{1,0:T(8,128)S(1)} copy-done((f32[32,100]{1,0:T(8,128)S(1)}, f32[32,100]{1,0:T(8,128)}, u32[]{:S(2)}) %copy-start.2) | copy-done | bytes 12824
  5.7 0.0 copy-start.3
  5.7 0.7 %copy-done.3 = f32[1024]{0:T(1024)S(1)} copy-done((f32[1024]{0:T(1024)S(1)}, f32[1024]{0:T(1024)}, u32[]{:S(2)}) %copy-start.3) | copy-done | bytes 4120
  6.3 0.0 copy-start.4
  6.3 0.7 %copy-done.4 = s32[2,4]{1,0:T(2,128)S(1)} copy-done((s32[2,4]{1,0:T(2,128)S(1)}, s32[2,4]{1,0:T(2,128)}, u32[]{:S(2)}) %copy-start.4) | copy-done | bytes 56
  7.0 52.6 %shard_map.103 = (f32[1,1]{1,0:T(1,128)}, bf16[4,32,1024]{2,1,0:T(8,128)(2,1)S(1)}, f32[1024,100]{1,0:T(8,128)S(1)}) custom-call(bf16[4,32,1024]{2,1,0:T(8,128)(2,1)S(1)} %copy-done.1, f32[1,1024]{1,0:T(1,128)S(1)} %bitcast.2, bf16[1024,3072]{1,0:T(8,128)(2,1)} %wqkv_hbm.1, bf16[1024,1024]{1,0:T(8,128)(2,1)S(1)} %copy-done, ...), custom_call_target="tpu_custom_call" | custom-call | tf_op jit(solution)/shard_map/pallas_call | solution.py:461
  59.6 1.0 %copy.12 = f32[1024,100]{0,1:T(8,128)} copy(f32[1024,100]{1,0:T(8,128)S(1)} %get-tuple-element.11) | data formatting | bytes 819200
  61.2 0.7 %copy.17 = bf16[4,32,1024]{2,1,0:T(8,128)(2,1)} copy(bf16[4,32,1024]{2,1,0:T(8,128)(2,1)S(1)} %get-tuple-element.16) | data formatting | bytes 524288
Async XLA Ops:
  2.4 1.6 %copy-start = (bf16[1024,1024]{1,0:T(8,128)(2,1)S(1)}, bf16[1024,1024]{1,0:T(8,128)(2,1)}, u32[]{:S(2)}) copy-start(bf16[1024,1024]{1,0:T(8,128)(2,1)} %wout_hbm.1) | copy-start | bytes 6291460
  4.0 0.9 %copy-start.1 = (bf16[4,32,1024]{2,1,0:T(8,128)(2,1)S(1)}, bf16[4,32,1024]{2,1,0:T(8,128)(2,1)}, u32[]{:S(2)}) copy-start(bf16[4,32,1024]{2,1,0:T(8,128)(2,1)} %states.1) | copy-start | bytes 786436
  4.9 0.7 %copy-start.2 = (f32[32,100]{1,0:T(8,128)S(1)}, f32[32,100]{1,0:T(8,128)}, u32[]{:S(2)}) copy-start(f32[32,100]{1,0:T(8,128)} %targets.1) | copy-start | bytes 38404
  5.7 0.7 %copy-start.3 = (f32[1024]{0:T(1024)S(1)}, f32[1024]{0:T(1024)}, u32[]{:S(2)}) copy-start(f32[1024]{0:T(1024)} %param.9) | copy-start | bytes 12292
  6.3 0.7 %copy-start.4 = (s32[2,4]{1,0:T(2,128)S(1)}, s32[2,4]{1,0:T(2,128)}, u32[]{:S(2)}) copy-start(s32[2,4]{1,0:T(2,128)} %neighbours.1) | copy-start | bytes 100
where the time goes:
time: 63.3 us; the launch traced here: 63 us
  Pallas kernels  52.6 us (83%)
  local copies, waits for them, and re-layouts  7.41 us (12%)
  between operations  3 us (5%)
    pallas_call x1, Pallas kernels, body(): pl.pallas_call(functools.partial(kernel, sizes), out_shape=(jax.ShapeDtyp...  52.6 us
    unnamed x13, local copies, waits for them, and re-layouts  7.41 us

commit v1 on v0

v1 whole, which is shorter than its diff:
```python
import functools

import jax
import jax.numpy as jnp
from jax import lax
from jax.experimental import pallas as pl
from jax.experimental.pallas import tpu as pltpu
from jax.sharding import PartitionSpec as P

HEADS = 16
VARS = 100
TILE = 16
EPS = 1e-05
DELTA = 0.1
LANES = 128
PACK = 4
VMEM_BYTES = 62 * 1024 * 1024
BLOCK = 256
MESH = pl.DeviceIdType.MESH
F32 = jnp.float32
BF16 = jnp.bfloat16

NN = (((1,), (0,)), ((), ()))
NT = (((1,), (1,)), ((), ()))
TN = (((0,), (0,)), ((), ()))


def dot(a, b, dims):
    return lax.dot_general(a, b, dims, preferred_element_type=F32)


def kernel(
    sizes,
    states_hbm,
    gain_hbm,
    wqkv_hbm,
    wout_hbm,
    whead_hbm,
    targets_hbm,
    neighbours_hbm,
    counts_hbm,
    loss,
    grad,
    head_out,
    states,
    gain,
    wqkv,
    wout,
    whead,
    targets,
    neighbours,
    counts,
    wpad,
    tpad,
    hall,
    query,
    kv,
    normed,
    inverse,
    cnt,
    hmask,
    probs,
    attn,
    mixed,
    ens,
    gradb,
    local,
    part,
    plane,
    full,
    dmixed,
    dmixedb,
    dattn,
    dquery,
    dkv,
    dsend,
    drecv,
    dhid,
    insem,
    wsem,
    halo_s,
    halo_r,
    pred_s,
    pred_r,
    part_s,
    part_r,
    plane_s,
    plane_r,
    full_s,
    full_r,
    back_s,
    back_r,
):
    n_member, n_y, n_z, n_core = sizes
    n_grid = n_y * n_z * n_core
    group = n_member * n_y * n_core
    members, points, width = states.shape
    window = hall.shape[1]
    flat = members * points
    cols = PACK * (width // HEADS)
    chunks = width // BLOCK
    packs = HEADS // PACK
    total_members = members * n_member
    per = local.shape[1]
    bands = width // LANES

    me_m = lax.axis_index("member")
    me_g = lax.axis_index("grid")
    core = lax.rem(me_g, n_core)
    me_z = lax.rem(me_g // n_core, n_z)
    me_y = me_g // (n_core * n_z)
    up = lax.rem(me_g + 1, n_grid)
    down = lax.rem(me_g + n_grid - 1, n_grid)
    mine = (me_m * n_y + me_y) * n_core + core

    def grid_at(y, z, c):
        return (y * n_z + z) * n_core + c

    def group_peer(k):
        m = lax.rem(me_m + k // (n_y * n_core), n_member)
        y = lax.rem(me_y + lax.rem(k // n_core, n_y), n_y)
        c = lax.rem(core + lax.rem(k, n_core), n_core)
        return (m, grid_at(y, me_z, c)), (m * n_y + y) * n_core + c

    def plane_peer(k):
        return (me_m, grid_at(me_y, lax.rem(me_z + k, n_z), core))

    barrier = pltpu.get_barrier_semaphore()

    def greet(device):
        pl.semaphore_signal(barrier, inc=1, device_id=device, device_id_type=MESH)

    def greet_group(k, c):
        greet(group_peer(k)[0])
        return c

    def greet_plane(k, c):
        greet(plane_peer(k))
        return c

    greet((me_m, up))
    greet((me_m, down))
    lax.fori_loop(1, n_z, greet_plane, 0)
    lax.fori_loop(1, group, greet_group, 0)

    wide = 2 * BLOCK
    n_wide = 3 * width // wide
    small_copies = [
        pltpu.make_async_copy(source, target, insem.at[i])
        for i, (source, target) in enumerate(
            (
                (states_hbm, states),
                (gain_hbm, gain),
                (neighbours_hbm, neighbours),
                (counts_hbm, counts),
                (whead_hbm, whead),
                (targets_hbm, targets),
            )
        )
    ]
    weight_copies = [
        pltpu.make_async_copy(
            wqkv_hbm.at[:, pl.ds(c * wide, wide)], wqkv.at[:, pl.ds(c * wide, wide)], wsem.at[c]
        )
        for c in range(n_wide)
    ]
    weight_copies.append(pltpu.make_async_copy(wout_hbm, wout, wsem.at[n_wide]))
    for copy in small_copies + weight_copies:
        copy.start()
    small_copies[0].wait()
    small_copies[1].wait()

    for m in range(members):
        values = states[m].astype(F32)
        centre = jnp.mean(values, axis=-1, keepdims=True)
        centred = values - centre
        spread = jnp.mean(centred * centred, axis=-1, keepdims=True)
        inv = lax.rsqrt(spread + EPS)
        norm = centred * inv
        normed[m] = norm
        inverse[m] = inv
        hall[m, pl.ds(points, points), :] = (norm * gain[...]).astype(BF16)

    pl.semaphore_wait(barrier, 2 + (group - 1) + (n_z - 1))

    own_rows = hall.at[:, pl.ds(points, points), :]
    halo = [
        pltpu.make_async_remote_copy(
            src_ref=own_rows,
            dst_ref=hall.at[:, pl.ds(start, points), :],
            send_sem=halo_s.at[i],
            recv_sem=halo_r.at[i],
            device_id=(me_m, side),
            device_id_type=MESH,
        )
        for i, (start, side) in enumerate(((0, up), (2 * points, down)))
    ]
    for copy in halo:
        copy.start()

    for copy in small_copies[2:]:
        copy.wait()

    key_tile = 2 * me_g - 2 + lax.broadcasted_iota(jnp.int32, (window, LANES), 0) // TILE
    lane = lax.broadcasted_iota(jnp.int32, (window, LANES), 1)
    query_tile = lax.rem(lane, points) // TILE
    number = jnp.zeros((window, LANES), F32)
    for t in range(points // TILE):
        for e in range(neighbours.shape[1]):
            hit = (key_tile == neighbours[t, e]) & (query_tile == t)
            number = number + jnp.where(hit, 1.0, 0.0)
    cnt[...] = number
    rows_i = lax.broadcasted_iota(jnp.int32, (PACK * points, cols), 0) // points
    cols_i = lax.broadcasted_iota(jnp.int32, (PACK * points, cols), 1) // (cols // PACK)
    hmask[...] = jnp.where(rows_i == cols_i, 1.0, 0.0)
    wpad[...] = jnp.zeros_like(wpad)
    wpad[pl.ds(0, VARS), :] = whead[...]
    tpad[...] = jnp.zeros_like(tpad)
    tpad[:, pl.ds(0, VARS)] = targets[...]

    own = hall[:, pl.ds(points, points), :].reshape(flat, width)
    for c in range(n_wide):
        weight_copies[c].wait()
        step = dot(own, wqkv[:, pl.ds(c * wide, wide)], NN).astype(BF16)
        if c * wide < width:
            query[:, pl.ds(c * wide, wide)] = step * jnp.asarray((width // HEADS) ** -0.5, BF16)
        else:
            there = pl.ds(c * wide - width, wide)
            kv[:, pl.ds(points, points), there] = step.reshape(members, points, wide)

    for copy in halo:
        copy.wait_recv()

    def keys_values(c, carry):
        here = pl.ds(pl.multiple_of(c * BLOCK, BLOCK), BLOCK)
        there = pl.ds(pl.multiple_of(width + c * BLOCK, BLOCK), BLOCK)
        rows = jnp.concatenate(
            [hall[:, pl.ds(0, points), :], hall[:, pl.ds(2 * points, points), :]], axis=0
        )
        step = dot(rows.reshape(2 * flat, width), wqkv[:, there], NN).astype(BF16)
        step = step.reshape(2, members, points, BLOCK)
        kv[:, pl.ds(0, points), here] = step[0]
        kv[:, pl.ds(2 * points, points), here] = step[1]
        return carry

    lax.fori_loop(0, 2 * width // BLOCK, keys_values, 0)

    def spread_heads(rows):
        return jnp.concatenate([rows] * PACK, axis=0) * hmask[...].astype(BF16)

    def pick_heads(rows):
        rows = rows * hmask[...]
        return jnp.sum(rows.reshape(PACK, points, cols), axis=0)

    pack_range = range(packs)
    heres = [pl.ds(h * cols, cols) for h in pack_range]
    theres = [pl.ds(width + h * cols, cols) for h in pack_range]

    def forward(m, carry):
        rows = pl.ds(pl.multiple_of(m * points, points), points)
        number = cnt[...]
        scores = [dot(kv[m, :, here], spread_heads(query[rows, here]), NT) for here in heres]
        scores = [jnp.where(number > 0.0, one, -3e38) for one in scores]
        tops = [jnp.max(one, axis=0, keepdims=True) for one in scores]
        expos = [jnp.exp(one - top) for one, top in zip(scores, tops)]
        totals = [jnp.sum(number * expo, axis=0, keepdims=True) for expo in expos]
        shares = [expo / total for expo, total in zip(expos, totals)]
        weights = [(number * one.astype(BF16).astype(F32)).astype(BF16) for one in shares]
        outs = [dot(one, kv[m, :, there], TN) for one, there in zip(weights, theres)]
        for h in pack_range:
            probs[m, h] = shares[h]
            attn[rows, heres[h]] = pick_heads(outs[h]).astype(BF16)
        return carry

    lax.fori_loop(0, members, forward, 0)
    weight_copies[n_wide].wait()

    flat_states = states[...].reshape(flat, width)
    for c in range(chunks):
        here = pl.ds(c * BLOCK, BLOCK)
        proj = dot(attn[...], wout[:, here], NN)
        mixed[:, here] = (flat_states[:, c * BLOCK : (c + 1) * BLOCK].astype(F32) + proj).astype(BF16)
    ens[0] = dot(mixed[...], wpad[...], NT).astype(BF16)

    def pred_copy(k):
        return pltpu.make_async_remote_copy(
            src_ref=ens.at[0],
            dst_ref=ens.at[k],
            send_sem=pred_s.at[k],
            recv_sem=pred_r.at[k],
            device_id=(lax.rem(me_m + k, n_member), me_g),
            device_id_type=MESH,
        )

    for k in range(1, n_member):
        pred_copy(k).start()

    row = lax.broadcasted_iota(jnp.int32, (points, LANES), 0)
    column = lax.broadcasted_iota(jnp.int32, (points, LANES), 1)
    valid = (row < counts[0]) & (column < VARS)

    def pair_sums(k, carry):
        def add(j, sums):
            other = ens[k, pl.ds(pl.multiple_of(j * points, points), points), :].astype(F32)
            pulls, apart = sums
            new = []
            for i in range(members):
                gap = ens[0, pl.ds(i * points, points), :].astype(F32) - other
                square = gap * gap + DELTA * DELTA
                root = lax.rsqrt(square)
                new.append(pulls[i] + gap * root)
                apart = apart + square * root
            return (tuple(new), apart)

        return lax.fori_loop(0, members, add, carry)

    blank = jnp.zeros((points, LANES), F32)
    sums = pair_sums(0, ((blank,) * members, blank))
    for k in sorted(range(1, n_member), key=lambda k: min(k, n_member - k)):
        pred_copy(k).wait_recv()
        sums = pair_sums(k, sums)
    pulls, apart = sums
    terms = (members * DELTA - apart) * (0.5 / (total_members - 1))
    for i in range(members):
        rows = pl.ds(i * points, points)
        miss = ens[0, rows, :].astype(F32) - tpad[...]
        square = miss * miss + DELTA * DELTA
        root = lax.rsqrt(square)
        slope = miss * root - pulls[i] * (1.0 / (total_members - 1))
        gradb[rows, :] = jnp.where(valid, slope, 0.0).astype(BF16)
        terms = terms + square * root
    terms = jnp.where(valid, terms, 0.0)
    loss_part = jnp.sum(jnp.sum(terms, axis=1, keepdims=True), axis=0, keepdims=True)

    tile_row = lax.broadcasted_iota(jnp.int32, (per, 32, LANES), 1)
    tile_at = mine * per + lax.broadcasted_iota(jnp.int32, (per, 32, LANES), 0)
    variable = (tile_at // bands) * 32 + tile_row
    spot = VARS % 32

    def split_loss(tiles):
        value = tiles[:, spot : spot + 1, :] + tiles[:, spot + 1 : spot + 2, :]
        high = value.astype(BF16).astype(F32)
        return jnp.where(
            variable == VARS, high, jnp.where(variable == VARS + 1, value - high, tiles)
        )

    row_all = lax.broadcasted_iota(jnp.int32, (LANES, 1), 0)
    loss_high = loss_part.astype(BF16).astype(F32)
    tail = jnp.where(
        row_all == VARS, loss_high, jnp.where(row_all == VARS + 1, loss_part - loss_high, 0.0)
    )
    for b in range(bands):
        band = dot(gradb[...], mixed[:, pl.ds(b * LANES, LANES)], TN) + tail
        for r in range(LANES // 32):
            t = r * bands + b
            local[t // per, t % per] = band[r * 32 : (r + 1) * 32].astype(BF16)

    def part_copy(k):
        device, owner = group_peer(k)
        return pltpu.make_async_remote_copy(
            src_ref=local.at[owner],
            dst_ref=part.at[k],
            send_sem=part_s.at[k],
            recv_sem=part_r.at[k],
            device_id=device,
            device_id_type=MESH,
        )

    def plane_copy(k):
        return pltpu.make_async_remote_copy(
            src_ref=plane.at[me_z],
            dst_ref=plane.at[me_z],
            send_sem=plane_s.at[k],
            recv_sem=plane_r.at[k],
            device_id=plane_peer(k),
            device_id_type=MESH,
        )

    def full_copy(k):
        return pltpu.make_async_remote_copy(
            src_ref=full.at[mine],
            dst_ref=full.at[mine],
            send_sem=full_s.at[k],
            recv_sem=full_r.at[k],
            device_id=group_peer(k)[0],
            device_id_type=MESH,
        )

    def each(count, make, act):
        def step(k, c):
            getattr(make(k), act)()
            return c

        lax.fori_loop(1, count, step, 0)

    each(group, part_copy, "start")

    for c in range(chunks):
        here = pl.ds(c * BLOCK, BLOCK)
        step = dot(gradb[...], wpad[:, here], NN)
        dmixed[:, here] = step
        dmixedb[:, here] = step.astype(BF16)
    for c in range(chunks):
        here = pl.ds(c * BLOCK, BLOCK)
        dattn[:, here] = dot(dmixedb[...], wout[here, :], NT).astype(BF16)

    scale = (width // HEADS) ** -0.5

    def backward(m, carry):
        rows = pl.ds(pl.multiple_of(m * points, points), points)
        number = cnt[...]
        outs = [spread_heads(dattn[rows, here]) for here in heres]
        dprobs = [dot(kv[m, :, there], out, NT) for there, out in zip(theres, outs)]
        shares = [probs[m, h] for h in pack_range]
        leans = [
            jnp.sum(number * one * share, axis=0, keepdims=True)
            for one, share in zip(dprobs, shares)
        ]
        dscores = [
            (share * (one - lean)).astype(BF16) for share, one, lean in zip(shares, dprobs, leans)
        ]
        dscores = [(number * one.astype(F32)).astype(BF16) for one in dscores]
        weights = [(number * one.astype(BF16).astype(F32)).astype(BF16) for one in shares]
        dqs = [dot(one, kv[m, :, here], TN) for one, here in zip(dscores, heres)]
        dks = [
            dot(one, spread_heads(query[rows, here]), NN) for one, here in zip(dscores, heres)
        ]
        dvs = [dot(one, out, NN) for one, out in zip(weights, outs)]
        for h in pack_range:
            dquery[rows, heres[h]] = (pick_heads(dqs[h]) * scale).astype(BF16)
            dkv[m, :, heres[h]] = dks[h].astype(BF16)
            dkv[m, :, theres[h]] = dvs[h].astype(BF16)
        return carry

    lax.fori_loop(0, members, backward, 0)

    def back_copy(side, c):
        return pltpu.make_async_remote_copy(
            src_ref=dsend.at[side, c],
            dst_ref=drecv.at[side, c],
            send_sem=back_s.at[side, c],
            recv_sem=back_r.at[side, c],
            device_id=(me_m, down if side == 0 else up),
            device_id_type=MESH,
        )

    for c in range(chunks):
        here = pl.ds(c * BLOCK, BLOCK)
        step = dot(dkv[...].reshape(members * window, 2 * width), wqkv[here, pl.ds(width, 2 * width)], NT)
        step = step.reshape(members, window, BLOCK)
        for side, start in ((0, 0), (1, 2 * points)):
            dsend[side, c] = step[:, start : start + points].astype(BF16)
            back_copy(side, c).start()
        dhid[:, :, here] = step[:, points : 2 * points]

    each(group, part_copy, "wait_recv")
    piece_sum = local[mine].astype(F32)
    for k in range(1, group):
        piece_sum = piece_sum + part[k].astype(F32)
    plane[me_z] = split_loss(piece_sum).astype(BF16)
    each(n_z, plane_copy, "start")

    for c in range(chunks):
        here = pl.ds(c * BLOCK, BLOCK)
        step = dot(dquery[...], wqkv[here, pl.ds(0, width)], NT)
        dhid[:, :, here] = dhid[:, :, here] + step.reshape(members, points, BLOCK)

    for c in range(chunks):
        here = pl.ds(c * BLOCK, BLOCK)
        for side in range(2):
            back_copy(side, c).wait_recv()
        extra = drecv[0, c].astype(F32) + drecv[1, c].astype(F32)
        dhid[:, :, here] = dhid[:, :, here] + extra

    for m in range(members):
        dnormed = dhid[m] * gain[...]
        norm = normed[m]
        first = jnp.mean(dnormed, axis=-1, keepdims=True)
        second = jnp.mean(dnormed * norm, axis=-1, keepdims=True)
        dstates = inverse[m] * (dnormed - first - norm * second)
        grad[m] = (dstates + dmixed[pl.ds(m * points, points), :]).astype(BF16)

    each(n_z, plane_copy, "wait_recv")
    plane_sum = plane[0].astype(F32)
    for k in range(1, n_z):
        plane_sum = plane_sum + plane[k].astype(F32)
    full[mine] = (split_loss(plane_sum) * (1.0 / (points * n_grid))).astype(BF16)
    each(group, full_copy, "start")
    each(group, full_copy, "wait_recv")
    for t in range(bands * LANES // 32):
        r, b = t // bands, t % bands
        count = min(32, VARS - 32 * r)
        here = (pl.ds(32 * r, count), pl.ds(b * LANES, LANES))
        head_out[here] = full[t // per, t % per][:count].astype(F32)
    t = (VARS // 32) * bands
    sums = full[t // per, t % per].astype(F32)
    total = sums[spot : spot + 1, 0:1] + sums[spot + 1 : spot + 2, 0:1]
    loss[...] = total * (1.0 / (VARS * total_members))

    for copy in halo:
        copy.wait_send()
    for k in range(1, n_member):
        pred_copy(k).wait_send()
    each(group, part_copy, "wait_send")
    each(n_z, plane_copy, "wait_send")
    each(group, full_copy, "wait_send")
    for c in range(chunks):
        for side in range(2):
            back_copy(side, c).wait_send()


def body(sizes, states, ln_gain, w_qkv, w_out, w_head, targets, neighbours, counts):
    n_member, n_y, n_z, n_core = sizes
    members, points, width = states.shape
    flat = members * points
    window = 3 * points
    group = n_member * n_y * n_core
    chunks = width // BLOCK
    cols = PACK * (width // HEADS)
    tiles = (LANES // 32) * (width // LANES)
    per = tiles // group
    vmem = pl.BlockSpec(memory_space=pltpu.VMEM)
    hbm = pl.BlockSpec(memory_space=pl.ANY)
    dma = pltpu.SemaphoreType.DMA
    loss, grad, head = pl.pallas_call(
        functools.partial(kernel, sizes),
        out_shape=(
            jax.ShapeDtypeStruct((1, 1), F32),
            jax.ShapeDtypeStruct((members, points, width), BF16),
            jax.ShapeDtypeStruct((VARS, width), F32),
        ),
        in_specs=[hbm] * 8,
        out_specs=(vmem, vmem, vmem),
        scratch_shapes=[
            pltpu.VMEM((members, points, width), BF16),
            pltpu.VMEM((1, width), F32),
            pltpu.VMEM((width, 3 * width), BF16),
            pltpu.VMEM((width, width), BF16),
            pltpu.VMEM((VARS, width), BF16),
            pltpu.VMEM((points, VARS), F32),
            pltpu.SMEM(neighbours.shape, jnp.int32),
            pltpu.SMEM((1,), jnp.int32),
            pltpu.VMEM((LANES, width), BF16),
            pltpu.VMEM((points, LANES), F32),
            pltpu.VMEM((members, window, width), BF16),
            pltpu.VMEM((flat, width), BF16),
            pltpu.VMEM((members, window, 2 * width), BF16),
            pltpu.VMEM((members, points, width), F32),
            pltpu.VMEM((members, points, 1), F32),
            pltpu.VMEM((window, LANES), F32),
            pltpu.VMEM((PACK * points, cols), F32),
            pltpu.VMEM((members, HEADS // PACK, window, PACK * points), F32),
            pltpu.VMEM((flat, width), BF16),
            pltpu.VMEM((flat, width), BF16),
            pltpu.VMEM((n_member, flat, LANES), BF16),
            pltpu.VMEM((flat, LANES), BF16),
            pltpu.VMEM((group, per, 32, LANES), BF16),
            pltpu.VMEM((group, per, 32, LANES), BF16),
            pltpu.VMEM((n_z, per, 32, LANES), BF16),
            pltpu.VMEM((group, per, 32, LANES), BF16),
            pltpu.VMEM((flat, width), F32),
            pltpu.VMEM((flat, width), BF16),
            pltpu.VMEM((flat, width), BF16),
            pltpu.VMEM((flat, width), BF16),
            pltpu.VMEM((members, window, 2 * width), BF16),
            pltpu.VMEM((2, chunks, members, points, BLOCK), BF16),
            pltpu.VMEM((2, chunks, members, points, BLOCK), BF16),
            pltpu.VMEM((members, points, width), F32),
            dma((6,)),
            dma((3 * width // (2 * BLOCK) + 1,)),
            dma((2,)),
            dma((2,)),
            dma((n_member,)),
            dma((n_member,)),
            dma((group,)),
            dma((group,)),
            dma((n_z,)),
            dma((n_z,)),
            dma((group,)),
            dma((group,)),
            dma((2, chunks)),
            dma((2, chunks)),
        ],
        compiler_params=pltpu.CompilerParams(
            collective_id=0, has_side_effects=True, vmem_limit_bytes=VMEM_BYTES
        ),
    )(states, ln_gain.reshape(1, width), w_qkv, w_out, w_head.T, targets, neighbours, counts)
    return (loss.reshape(()), grad, head.T)


def solution(mesh):
    placed = (
        P("member", "grid", None),
        P(),
        P(),
        P(),
        P(),
        P("grid", None),
        P("grid", None),
        P("grid"),
    )
    n_core = 2
    n_z = min(8, mesh.shape["grid"] // n_core)
    sizes = (mesh.shape["member"], mesh.shape["grid"] // (n_z * n_core), n_z, n_core)
    return jax.shard_map(
        functools.partial(body, sizes),
        mesh=mesh,
        in_specs=placed,
        out_specs=(P(), P("member", "grid", None), P()),
        check_vma=False,
    )
```

time: 63.3 us -> 55.8 us (0.88)
  local copies, waits for them, and re-layouts: 7.41 us -> 3.46 us
  Pallas kernels: 52.6 us -> 49.2 us
    unnamed x13 -> x2, local copies, waits for them, and re-layouts: 7.41 us -> 3.46 us
    pallas_call x1, Pallas kernels: 52.6 us -> 49.2 us  [body(): pl.pallas_call(functools.partial(kernel, sizes), out_shape=(jax.ShapeDtyp...]
where the time goes in v1:
time: 55.8 us; the launch traced here: 55.6 us
  Pallas kernels  49.2 us (88%)
  local copies, waits for them, and re-layouts  3.46 us (6%)
  between operations  2.99 us (5%)
    pallas_call x1, Pallas kernels, body(): pl.pallas_call(functools.partial(kernel, sizes), out_shape=(jax.ShapeDtyp...  49.2 us
    unnamed x2, local copies, waits for them, and re-layouts  3.46 us

profile of v1, /device:TPU:1, one launch (start us, length us, event | category | flops | bytes accessed | tf_op | source)
XLA Modules:
  0.0 55.6 jit_solution(10629731887866138382)
XLA Ops:
  1.3 49.2 %shard_map.103 = (f32[1,1]{1,0:T(1,128)}, bf16[4,32,1024]{2,1,0:T(8,128)(2,1)}, f32[100,1024]{1,0:T(8,128)}) custom-call(bf16[4,32,1024]{2,1,0:T(8,128)(2,1)} %states_hbm.1, f32[1,1024]{1,0:T(1,128)} %bitcast.6, bf16[1024,3072]{1,0:T(8,128)(2,1)} %wqkv_hbm.1, bf16[1024,1024]{1,0:T(8,128)(2,1)} %wout_hbm.1, bf16[100,1024]{1,0:T(8,128)(2,1)} %bitcast.5, ...), custom_call_target="tpu_custom_call" | custom-call | tf_op jit(solution)/shard_map/pallas_call | solution.py:525
  51.0 1.7 %copy.16 = bf16[4,32,1024]{2,1,0:T(8,128)(2,1)} copy(bf16[4,32,1024]{2,1,0:T(8,128)(2,1)} %get-tuple-element.13) | data formatting | bytes 524288
  52.7 1.8 %copy.17 = f32[1024,100]{0,1:T(8,128)} copy(f32[1024,100]{0,1:T(8,128)} %bitcast.4) | data formatting | bytes 819200

commit v2 on v1

--- a/solution.py
+++ b/solution.py
@@ -14,7 +14,7 @@
 DELTA = 0.1
 LANES = 128
 PACK = 4
-VMEM_BYTES = 62 * 1024 * 1024
+VMEM_BYTES = 40 * 1024 * 1024
 BLOCK = 256
 MESH = pl.DeviceIdType.MESH
 F32 = jnp.float32
@@ -52,7 +52,8 @@
     counts,
     wpad,
     tpad,
-    hall,
+    hidden,
+    beside,
     query,
     kv,
     normed,
@@ -95,7 +96,7 @@
     n_grid = n_y * n_z * n_core
     group = n_member * n_y * n_core
     members, points, width = states.shape
-    window = hall.shape[1]
+    window = kv.shape[1]
     flat = members * points
     cols = PACK * (width // HEADS)
     chunks = width // BLOCK
@@ -179,21 +180,20 @@
         norm = centred * inv
         normed[m] = norm
         inverse[m] = inv
-        hall[m, pl.ds(points, points), :] = (norm * gain[...]).astype(BF16)
+        hidden[pl.ds(m * points, points), :] = (norm * gain[...]).astype(BF16)
 
     pl.semaphore_wait(barrier, 2 + (group - 1) + (n_z - 1))
 
-    own_rows = hall.at[:, pl.ds(points, points), :]
     halo = [
         pltpu.make_async_remote_copy(
-            src_ref=own_rows,
-            dst_ref=hall.at[:, pl.ds(start, points), :],
+            src_ref=hidden,
+            dst_ref=beside.at[i],
             send_sem=halo_s.at[i],
             recv_sem=halo_r.at[i],
             device_id=(me_m, side),
             device_id_type=MESH,
         )
-        for i, (start, side) in enumerate(((0, up), (2 * points, down)))
+        for i, side in enumerate((up, down))
     ]
     for copy in halo:
         copy.start()
@@ -218,10 +218,9 @@
     tpad[...] = jnp.zeros_like(tpad)
     tpad[:, pl.ds(0, VARS)] = targets[...]
 
-    own = hall[:, pl.ds(points, points), :].reshape(flat, width)
     for c in range(n_wide):
         weight_copies[c].wait()
-        step = dot(own, wqkv[:, pl.ds(c * wide, wide)], NN).astype(BF16)
+        step = dot(hidden[...], wqkv[:, pl.ds(c * wide, wide)], NN).astype(BF16)
         if c * wide < width:
             query[:, pl.ds(c * wide, wide)] = step * jnp.asarray((width // HEADS) ** -0.5, BF16)
         else:
@@ -231,19 +230,12 @@
     for copy in halo:
         copy.wait_recv()
 
-    def keys_values(c, carry):
-        here = pl.ds(pl.multiple_of(c * BLOCK, BLOCK), BLOCK)
-        there = pl.ds(pl.multiple_of(width + c * BLOCK, BLOCK), BLOCK)
-        rows = jnp.concatenate(
-            [hall[:, pl.ds(0, points), :], hall[:, pl.ds(2 * points, points), :]], axis=0
-        )
-        step = dot(rows.reshape(2 * flat, width), wqkv[:, there], NN).astype(BF16)
-        step = step.reshape(2, members, points, BLOCK)
+    for c in range(2 * width // wide):
+        here = pl.ds(c * wide, wide)
+        step = dot(beside[...].reshape(2 * flat, width), wqkv[:, pl.ds(width + c * wide, wide)], NN)
+        step = step.astype(BF16).reshape(2, members, points, wide)
         kv[:, pl.ds(0, points), here] = step[0]
         kv[:, pl.ds(2 * points, points), here] = step[1]
-        return carry
-
-    lax.fori_loop(0, 2 * width // BLOCK, keys_values, 0)
 
     def spread_heads(rows):
         return jnp.concatenate([rows] * PACK, axis=0) * hmask[...].astype(BF16)
@@ -386,6 +378,12 @@
             device_id_type=MESH,
         )
 
+    def apart_by(k):
+        m, y = k // (n_y * n_core), k // n_core % n_y
+        return min(m, n_member - m) + min(y, n_y - y)
+
+    far_first = sorted(range(1, group), key=lambda k: -apart_by(k))
+
     def each(count, make, act):
         def step(k, c):
             getattr(make(k), act)()
@@ -393,7 +391,8 @@
 
         lax.fori_loop(1, count, step, 0)
 
-    each(group, part_copy, "start")
+    for k in far_first:
+        part_copy(k).start()
 
     for c in range(chunks):
         here = pl.ds(c * BLOCK, BLOCK)
@@ -485,7 +484,8 @@
     for k in range(1, n_z):
         plane_sum = plane_sum + plane[k].astype(F32)
     full[mine] = (split_loss(plane_sum) * (1.0 / (points * n_grid))).astype(BF16)
-    each(group, full_copy, "start")
+    for k in far_first:
+        full_copy(k).start()
     each(group, full_copy, "wait_recv")
     for t in range(bands * LANES // 32):
         r, b = t // bands, t % bands
@@ -522,6 +522,7 @@
     vmem = pl.BlockSpec(memory_space=pltpu.VMEM)
     hbm = pl.BlockSpec(memory_space=pl.ANY)
     dma = pltpu.SemaphoreType.DMA
+    operands = (states, ln_gain.reshape(1, width), w_qkv, w_out, w_head.T, targets, neighbours, counts)
     loss, grad, head = pl.pallas_call(
         functools.partial(kernel, sizes),
         out_shape=(
@@ -542,7 +543,8 @@
             pltpu.SMEM((1,), jnp.int32),
             pltpu.VMEM((LANES, width), BF16),
             pltpu.VMEM((points, LANES), F32),
-            pltpu.VMEM((members, window, width), BF16),
+            pltpu.VMEM((flat, width), BF16),
+            pltpu.VMEM((2, flat, width), BF16),
             pltpu.VMEM((flat, width), BF16),
             pltpu.VMEM((members, window, 2 * width), BF16),
             pltpu.VMEM((members, points, width), F32),
@@ -584,7 +586,7 @@
         compiler_params=pltpu.CompilerParams(
             collective_id=0, has_side_effects=True, vmem_limit_bytes=VMEM_BYTES
         ),
-    )(states, ln_gain.reshape(1, width), w_qkv, w_out, w_head.T, targets, neighbours, counts)
+    )(*(pltpu.with_memory_space_constraint(x, pltpu.HBM) for x in operands[:-1]), operands[-1])
     return (loss.reshape(()), grad, head.T)
 
 

time: 55.8 us -> 50.5 us (0.905)
  Pallas kernels: 49.2 us -> 45.9 us
  local copies, waits for them, and re-layouts: 3.46 us -> 1.46 us
    pallas_call x1, Pallas kernels: 49.2 us -> 45.9 us  [body(): pl.pallas_call(functools.partial(kernel, sizes), out_shape=(jax.ShapeDtyp...]
    unnamed x2, local copies, waits for them, and re-layouts: 3.46 us -> 1.46 us
where the time goes in v2:
time: 50.5 us; the launch traced here: 50.4 us
  Pallas kernels  45.9 us (91%)
  between operations  2.97 us (6%)
  local copies, waits for them, and re-layouts  1.46 us (3%)
    pallas_call x1, Pallas kernels, body(): pl.pallas_call(functools.partial(kernel, sizes), out_shape=(jax.ShapeDtyp...  45.9 us
    unnamed x2, local copies, waits for them, and re-layouts  1.46 us

profile of v2, /device:TPU:1, one launch (start us, length us, event | category | flops | bytes accessed | tf_op | source)
XLA Modules:
  0.0 50.4 jit_solution(16008460692380351938)
XLA Ops:
  1.3 45.9 %shard_map.103 = (f32[1,1]{1,0:T(1,128)}, bf16[4,32,1024]{2,1,0:T(8,128)(2,1)S(1)}, f32[100,1024]{1,0:T(8,128)S(1)}) custom-call(bf16[4,32,1024]{2,1,0:T(8,128)(2,1)} %states_hbm.1, f32[1,1024]{1,0:T(1,128)} %bitcast.6, bf16[1024,3072]{1,0:T(8,128)(2,1)} %wqkv_hbm.1, bf16[1024,1024]{1,0:T(8,128)(2,1)} %wout_hbm.1, bf16[100,1024]{1,0:T(8,128)(2,1)} %bitcast.5, ...), custom_call_target="tpu_custom_call" | custom-call | tf_op jit(solution)/shard_map/pallas_call | solution.py:526
  47.8 0.7 %copy.16 = bf16[4,32,1024]{2,1,0:T(8,128)(2,1)} copy(bf16[4,32,1024]{2,1,0:T(8,128)(2,1)S(1)} %get-tuple-element.13) | data formatting | bytes 524288
  48.5 0.8 %copy.17 = f32[1024,100]{0,1:T(8,128)} copy(f32[1024,100]{0,1:T(8,128)S(1)} %bitcast.4) | data formatting | bytes 819200

commit v3 on v2

--- a/solution.py
+++ b/solution.py
@@ -14,6 +14,7 @@
 DELTA = 0.1
 LANES = 128
 PACK = 4
+HALVES = 2
 VMEM_BYTES = 40 * 1024 * 1024
 BLOCK = 256
 MESH = pl.DeviceIdType.MESH
@@ -63,7 +64,11 @@
     probs,
     attn,
     mixed,
+    mix,
     ens,
+    pens,
+    slopes,
+    gradall,
     gradb,
     local,
     part,
@@ -83,6 +88,8 @@
     halo_r,
     pred_s,
     pred_r,
+    mix_s,
+    mix_r,
     part_s,
     part_r,
     plane_s,
@@ -104,6 +111,8 @@
     total_members = members * n_member
     per = local.shape[1]
     bands = width // LANES
+    parts = n_y * n_core
+    held = n_member * members
 
     me_m = lax.axis_index("member")
     me_g = lax.axis_index("grid")
@@ -112,7 +121,8 @@
     me_y = me_g // (n_core * n_z)
     up = lax.rem(me_g + 1, n_grid)
     down = lax.rem(me_g + n_grid - 1, n_grid)
-    mine = (me_m * n_y + me_y) * n_core + core
+    my_part = me_y * n_core + core
+    mine = me_m * parts + my_part
 
     def grid_at(y, z, c):
         return (y * n_z + z) * n_core + c
@@ -121,7 +131,12 @@
         m = lax.rem(me_m + k // (n_y * n_core), n_member)
         y = lax.rem(me_y + lax.rem(k // n_core, n_y), n_y)
         c = lax.rem(core + lax.rem(k, n_core), n_core)
-        return (m, grid_at(y, me_z, c)), (m * n_y + y) * n_core + c
+        return (m, grid_at(y, me_z, c))
+
+    def part_peer(k):
+        y = lax.rem(me_y + k // n_core, n_y)
+        c = lax.rem(core + lax.rem(k, n_core), n_core)
+        return (me_m, grid_at(y, me_z, c)), y * n_core + c
 
     def plane_peer(k):
         return (me_m, grid_at(me_y, lax.rem(me_z + k, n_z), core))
@@ -132,7 +147,7 @@
         pl.semaphore_signal(barrier, inc=1, device_id=device, device_id_type=MESH)
 
     def greet_group(k, c):
-        greet(group_peer(k)[0])
+        greet(group_peer(k))
         return c
 
     def greet_plane(k, c):
@@ -184,19 +199,25 @@
 
     pl.semaphore_wait(barrier, 2 + (group - 1) + (n_z - 1))
 
+    some = members // HALVES
+    band_rows = [pl.ds(h * some * points, some * points) for h in range(HALVES)]
     halo = [
-        pltpu.make_async_remote_copy(
-            src_ref=hidden,
-            dst_ref=beside.at[i],
-            send_sem=halo_s.at[i],
-            recv_sem=halo_r.at[i],
-            device_id=(me_m, side),
-            device_id_type=MESH,
-        )
-        for i, side in enumerate((up, down))
+        [
+            pltpu.make_async_remote_copy(
+                src_ref=hidden.at[rows],
+                dst_ref=beside.at[i, rows],
+                send_sem=halo_s.at[h, i],
+                recv_sem=halo_r.at[h, i],
+                device_id=(me_m, side),
+                device_id_type=MESH,
+            )
+            for i, side in enumerate((up, down))
+        ]
+        for h, rows in enumerate(band_rows)
     ]
-    for copy in halo:
-        copy.start()
+    for pair in halo:
+        for copy in pair:
+            copy.start()
 
     for copy in small_copies[2:]:
         copy.wait()
@@ -227,16 +248,6 @@
             there = pl.ds(c * wide - width, wide)
             kv[:, pl.ds(points, points), there] = step.reshape(members, points, wide)
 
-    for copy in halo:
-        copy.wait_recv()
-
-    for c in range(2 * width // wide):
-        here = pl.ds(c * wide, wide)
-        step = dot(beside[...].reshape(2 * flat, width), wqkv[:, pl.ds(width + c * wide, wide)], NN)
-        step = step.astype(BF16).reshape(2, members, points, wide)
-        kv[:, pl.ds(0, points), here] = step[0]
-        kv[:, pl.ds(2 * points, points), here] = step[1]
-
     def spread_heads(rows):
         return jnp.concatenate([rows] * PACK, axis=0) * hmask[...].astype(BF16)
 
@@ -248,85 +259,126 @@
     heres = [pl.ds(h * cols, cols) for h in pack_range]
     theres = [pl.ds(width + h * cols, cols) for h in pack_range]
 
-    def forward(m, carry):
-        rows = pl.ds(pl.multiple_of(m * points, points), points)
-        number = cnt[...]
-        scores = [dot(kv[m, :, here], spread_heads(query[rows, here]), NT) for here in heres]
+    share = chunks // n_member
+
+    def mix_copy(h, k):
+        return pltpu.make_async_remote_copy(
+            src_ref=mixed.at[pl.ds(lax.rem(me_m + k, n_member) * share, share), band_rows[h]],
+            dst_ref=mix.at[k, :, band_rows[h]],
+            send_sem=mix_s.at[h, k],
+            recv_sem=mix_r.at[h, k],
+            device_id=(lax.rem(me_m + k, n_member), me_g),
+            device_id_type=MESH,
+        )
+
+    def pred_copy(h, k):
+        return pltpu.make_async_remote_copy(
+            src_ref=ens.at[0, band_rows[h]],
+            dst_ref=ens.at[k, band_rows[h]],
+            send_sem=pred_s.at[h, k],
+            recv_sem=pred_r.at[h, k],
+            device_id=(lax.rem(me_m + k, n_member), me_g),
+            device_id_type=MESH,
+        )
+
+    far_members = sorted(range(1, n_member), key=lambda k: -min(k, n_member - k))
+    number = cnt[...]
+    for h in range(HALVES):
+        for copy in halo[h]:
+            copy.wait_recv()
+        near = beside[:, band_rows[h], :].reshape(2 * some * points, width)
+        group_members = pl.ds(h * some, some)
+        for c in range(2 * width // wide):
+            here = pl.ds(c * wide, wide)
+            step = dot(near, wqkv[:, pl.ds(width + c * wide, wide)], NN)
+            step = step.astype(BF16).reshape(2, some, points, wide)
+            kv[group_members, pl.ds(0, points), here] = step[0]
+            kv[group_members, pl.ds(2 * points, points), here] = step[1]
+
+        pairs = [(m, p) for m in range(h * some, (h + 1) * some) for p in pack_range]
+        queries = [query[pl.ds(m * points, points), heres[p]] for m, p in pairs]
+        scores = [dot(kv[m, :, heres[p]], spread_heads(q), NT) for (m, p), q in zip(pairs, queries)]
         scores = [jnp.where(number > 0.0, one, -3e38) for one in scores]
         tops = [jnp.max(one, axis=0, keepdims=True) for one in scores]
         expos = [jnp.exp(one - top) for one, top in zip(scores, tops)]
         totals = [jnp.sum(number * expo, axis=0, keepdims=True) for expo in expos]
         shares = [expo / total for expo, total in zip(expos, totals)]
         weights = [(number * one.astype(BF16).astype(F32)).astype(BF16) for one in shares]
-        outs = [dot(one, kv[m, :, there], TN) for one, there in zip(weights, theres)]
-        for h in pack_range:
-            probs[m, h] = shares[h]
-            attn[rows, heres[h]] = pick_heads(outs[h]).astype(BF16)
-        return carry
-
-    lax.fori_loop(0, members, forward, 0)
-    weight_copies[n_wide].wait()
-
-    flat_states = states[...].reshape(flat, width)
-    for c in range(chunks):
-        here = pl.ds(c * BLOCK, BLOCK)
-        proj = dot(attn[...], wout[:, here], NN)
-        mixed[:, here] = (flat_states[:, c * BLOCK : (c + 1) * BLOCK].astype(F32) + proj).astype(BF16)
-    ens[0] = dot(mixed[...], wpad[...], NT).astype(BF16)
-
-    def pred_copy(k):
-        return pltpu.make_async_remote_copy(
-            src_ref=ens.at[0],
-            dst_ref=ens.at[k],
-            send_sem=pred_s.at[k],
-            recv_sem=pred_r.at[k],
-            device_id=(lax.rem(me_m + k, n_member), me_g),
-            device_id_type=MESH,
-        )
-
-    for k in range(1, n_member):
-        pred_copy(k).start()
-
-    row = lax.broadcasted_iota(jnp.int32, (points, LANES), 0)
-    column = lax.broadcasted_iota(jnp.int32, (points, LANES), 1)
-    valid = (row < counts[0]) & (column < VARS)
-
-    def pair_sums(k, carry):
-        def add(j, sums):
-            other = ens[k, pl.ds(pl.multiple_of(j * points, points), points), :].astype(F32)
-            pulls, apart = sums
-            new = []
-            for i in range(members):
-                gap = ens[0, pl.ds(i * points, points), :].astype(F32) - other
+        outs = [dot(one, kv[m, :, theres[p]], TN) for one, (m, p) in zip(weights, pairs)]
+        for (m, p), one, out in zip(pairs, shares, outs):
+            probs[m, p] = one
+            attn[pl.ds(m * points, points), heres[p]] = pick_heads(out).astype(BF16)
+
+        if h == 0:
+            weight_copies[n_wide].wait()
+        rows = band_rows[h]
+        for k in (*far_members, 0):
+            for c in range(share):
+                block = lax.rem(me_m + k, n_member) * share + c
+                here = pl.ds(pl.multiple_of(block * BLOCK, BLOCK), BLOCK)
+                proj = dot(attn[rows, :], wout[:, here], NN)
+                before = states[group_members, :, here].reshape(some * points, BLOCK).astype(F32)
+                mixed[block, rows] = (before + proj).astype(BF16)
+            if k != 0 and (h < HALVES - 1 or k == far_members[0]):
+                mix_copy(h, k).start()
+        pred = dot(mixed[0, rows], wpad[:, pl.ds(0, BLOCK)], NT)
+        for c in range(1, chunks):
+            pred = pred + dot(mixed[c, rows], wpad[:, pl.ds(c * BLOCK, BLOCK)], NT)
+        ens[0, rows] = pred.astype(BF16)
+        for k in far_members:
+            pred_copy(h, k).start()
+        if h == HALVES - 1:
+            for k in far_members[1:]:
+                mix_copy(h, k).start()
+    mix[0] = mixed[pl.ds(me_m * share, share)]
+    for h in range(HALVES):
+        for k in range(1, n_member):
+            pred_copy(h, k).wait_recv()
+
+    step_rows = 8
+
+    def crps(block, total):
+        start = pl.multiple_of(block * step_rows, step_rows)
+        row = start + lax.broadcasted_iota(jnp.int32, (step_rows, LANES), 0)
+        column = lax.broadcasted_iota(jnp.int32, (step_rows, LANES), 1)
+        valid = (row < counts[0]) & (column < VARS)
+        target = tpad[pl.ds(start, step_rows), :]
+        values = [pens[i, pl.ds(start, step_rows), :] for i in range(held)]
+        pulls = [None] * held
+        apart = jnp.zeros((step_rows, LANES), F32)
+        for i in range(held):
+            for j in range(i + 1, held):
+                gap = values[i] - values[j]
                 square = gap * gap + DELTA * DELTA
                 root = lax.rsqrt(square)
-                new.append(pulls[i] + gap * root)
-                apart = apart + square * root
-            return (tuple(new), apart)
-
-        return lax.fori_loop(0, members, add, carry)
-
-    blank = jnp.zeros((points, LANES), F32)
-    sums = pair_sums(0, ((blank,) * members, blank))
-    for k in sorted(range(1, n_member), key=lambda k: min(k, n_member - k)):
-        pred_copy(k).wait_recv()
-        sums = pair_sums(k, sums)
-    pulls, apart = sums
-    terms = (members * DELTA - apart) * (0.5 / (total_members - 1))
-    for i in range(members):
-        rows = pl.ds(i * points, points)
-        miss = ens[0, rows, :].astype(F32) - tpad[...]
-        square = miss * miss + DELTA * DELTA
-        root = lax.rsqrt(square)
-        slope = miss * root - pulls[i] * (1.0 / (total_members - 1))
-        gradb[rows, :] = jnp.where(valid, slope, 0.0).astype(BF16)
-        terms = terms + square * root
-    terms = jnp.where(valid, terms, 0.0)
+                pull = gap * root
+                pulls[i] = pull if pulls[i] is None else pulls[i] + pull
+                pulls[j] = -pull if pulls[j] is None else pulls[j] - pull
+                if i < members:
+                    length = square * root
+                    apart = apart + (length + length if j < members else length)
+        terms = apart * (-0.5 / (total_members - 1))
+        for i in range(held):
+            miss = values[i] - target
+            square = miss * miss + DELTA * DELTA
+            root = lax.rsqrt(square)
+            slope = miss * root - pulls[i] * (1.0 / (total_members - 1))
+            slopes[i, pl.ds(start, step_rows), :] = jnp.where(valid, slope, 0.0)
+            if i < members:
+                terms = terms + square * root
+        return total + jnp.where(valid, terms, 0.0)
+
+    for k in range(n_member):
+        pens[pl.ds(k * members, members)] = ens[k].astype(F32).reshape(members, points, LANES)
+    terms = lax.fori_loop(0, points // step_rows, crps, jnp.zeros((step_rows, LANES), F32))
     loss_part = jnp.sum(jnp.sum(terms, axis=1, keepdims=True), axis=0, keepdims=True)
-
+    gradall[...] = slopes[...].reshape(held * points, LANES).astype(BF16)
+    gradb[...] = gradall[pl.ds(0, flat), :]
+
+    quads = LANES // 32
     tile_row = lax.broadcasted_iota(jnp.int32, (per, 32, LANES), 1)
-    tile_at = mine * per + lax.broadcasted_iota(jnp.int32, (per, 32, LANES), 0)
-    variable = (tile_at // bands) * 32 + tile_row
+    tile_at = my_part * per + lax.broadcasted_iota(jnp.int32, (per, 32, LANES), 0)
+    variable = lax.rem(tile_at, quads) * 32 + tile_row
     spot = VARS % 32
 
     def split_loss(tiles):
@@ -341,14 +393,21 @@
     tail = jnp.where(
         row_all == VARS, loss_high, jnp.where(row_all == VARS + 1, loss_part - loss_high, 0.0)
     )
-    for b in range(bands):
-        band = dot(gradb[...], mixed[:, pl.ds(b * LANES, LANES)], TN) + tail
-        for r in range(LANES // 32):
-            t = r * bands + b
-            local[t // per, t % per] = band[r * 32 : (r + 1) * 32].astype(BF16)
+    for h in range(HALVES):
+        for k in range(1, n_member):
+            mix_copy(h, k).wait_recv()
+    per_block = BLOCK // LANES
+    for c in range(share):
+        block = dot(gradall[...], mix[:, c].reshape(held * points, BLOCK), TN) + tail
+        for b in range(per_block):
+            for r in range(quads):
+                u = (c * per_block + b) * quads + r
+                local[u // per, u % per] = block[
+                    r * 32 : (r + 1) * 32, b * LANES : (b + 1) * LANES
+                ].astype(BF16)
 
     def part_copy(k):
-        device, owner = group_peer(k)
+        device, owner = part_peer(k)
         return pltpu.make_async_remote_copy(
             src_ref=local.at[owner],
             dst_ref=part.at[k],
@@ -374,7 +433,7 @@
             dst_ref=full.at[mine],
             send_sem=full_s.at[k],
             recv_sem=full_r.at[k],
-            device_id=group_peer(k)[0],
+            device_id=group_peer(k),
             device_id_type=MESH,
         )
 
@@ -391,7 +450,7 @@
 
         lax.fori_loop(1, count, step, 0)
 
-    for k in far_first:
+    for k in range(parts - 1, 0, -1):
         part_copy(k).start()
 
     for c in range(chunks):
@@ -443,7 +502,18 @@
             device_id_type=MESH,
         )
 
+    def second_stage():
+        each(parts, part_copy, "wait_recv")
+        piece_sum = local[my_part].astype(F32)
+        for k in range(1, parts):
+            piece_sum = piece_sum + part[k].astype(F32)
+        plane[me_z] = split_loss(piece_sum).astype(BF16)
+        for k in sorted(range(1, n_z), key=lambda k: -min(k, n_z - k)):
+            plane_copy(k).start()
+
     for c in range(chunks):
+        if c == chunks // 2:
+            second_stage()
         here = pl.ds(c * BLOCK, BLOCK)
         step = dot(dkv[...].reshape(members * window, 2 * width), wqkv[here, pl.ds(width, 2 * width)], NT)
         step = step.reshape(members, window, BLOCK)
@@ -452,18 +522,18 @@
             back_copy(side, c).start()
         dhid[:, :, here] = step[:, points : 2 * points]
 
-    each(group, part_copy, "wait_recv")
-    piece_sum = local[mine].astype(F32)
-    for k in range(1, group):
-        piece_sum = piece_sum + part[k].astype(F32)
-    plane[me_z] = split_loss(piece_sum).astype(BF16)
-    each(n_z, plane_copy, "start")
-
     for c in range(chunks):
         here = pl.ds(c * BLOCK, BLOCK)
         step = dot(dquery[...], wqkv[here, pl.ds(0, width)], NT)
         dhid[:, :, here] = dhid[:, :, here] + step.reshape(members, points, BLOCK)
 
+    each(n_z, plane_copy, "wait_recv")
+    plane_sum = plane[0].astype(F32)
+    for k in range(1, n_z):
+        plane_sum = plane_sum + plane[k].astype(F32)
+    full[mine] = (split_loss(plane_sum) * (1.0 / (points * n_grid))).astype(BF16)
+    for k in far_first:
+        full_copy(k).start()
     for c in range(chunks):
         here = pl.ds(c * BLOCK, BLOCK)
         for side in range(2):
@@ -479,34 +549,41 @@
         dstates = inverse[m] * (dnormed - first - norm * second)
         grad[m] = (dstates + dmixed[pl.ds(m * points, points), :]).astype(BF16)
 
-    each(n_z, plane_copy, "wait_recv")
-    plane_sum = plane[0].astype(F32)
-    for k in range(1, n_z):
-        plane_sum = plane_sum + plane[k].astype(F32)
-    full[mine] = (split_loss(plane_sum) * (1.0 / (points * n_grid))).astype(BF16)
-    for k in far_first:
-        full_copy(k).start()
     each(group, full_copy, "wait_recv")
-    for t in range(bands * LANES // 32):
-        r, b = t // bands, t % bands
-        count = min(32, VARS - 32 * r)
-        here = (pl.ds(32 * r, count), pl.ds(b * LANES, LANES))
-        head_out[here] = full[t // per, t % per][:count].astype(F32)
-    t = (VARS // 32) * bands
-    sums = full[t // per, t % per].astype(F32)
-    total = sums[spot : spot + 1, 0:1] + sums[spot + 1 : spot + 2, 0:1]
+    total = jnp.zeros((1, 1), F32)
+    for m in range(n_member):
+        for u in range(parts * per):
+            b, r = m * (bands // n_member) + u // quads, u % quads
+            tile = full[m * parts + u // per, u % per].astype(F32)
+            count = min(32, VARS - 32 * r)
+            head_out[pl.ds(32 * r, count), pl.ds(b * LANES, LANES)] = tile[:count]
+            if u == VARS // 32:
+                total = total + tile[spot : spot + 1, 0:1] + tile[spot + 1 : spot + 2, 0:1]
     loss[...] = total * (1.0 / (VARS * total_members))
 
-    for copy in halo:
-        copy.wait_send()
-    for k in range(1, n_member):
-        pred_copy(k).wait_send()
-    each(group, part_copy, "wait_send")
+    for h in range(HALVES):
+        for copy in halo[h]:
+            copy.wait_send()
+        for k in range(1, n_member):
+            pred_copy(h, k).wait_send()
+            mix_copy(h, k).wait_send()
+    each(parts, part_copy, "wait_send")
     each(n_z, plane_copy, "wait_send")
     each(group, full_copy, "wait_send")
     for c in range(chunks):
         for side in range(2):
             back_copy(side, c).wait_send()
+
+
+def results(loss, grad, head, loss_hbm, grad_hbm, head_hbm, sem):
+    copies = [
+        pltpu.make_async_copy(source, target, sem.at[i])
+        for i, (source, target) in enumerate(((grad, grad_hbm), (head, head_hbm), (loss, loss_hbm)))
+    ]
+    for copy in copies:
+        copy.start()
+    for copy in copies:
+        copy.wait()
 
 
 def body(sizes, states, ln_gain, w_qkv, w_out, w_head, targets, neighbours, counts):
@@ -553,11 +630,15 @@
             pltpu.VMEM((PACK * points, cols), F32),
             pltpu.VMEM((members, HEADS // PACK, window, PACK * points), F32),
             pltpu.VMEM((flat, width), BF16),
-            pltpu.VMEM((flat, width), BF16),
+            pltpu.VMEM((chunks, flat, BLOCK), BF16),
+            pltpu.VMEM((n_member, chunks // n_member, flat, BLOCK), BF16),
             pltpu.VMEM((n_member, flat, LANES), BF16),
+            pltpu.VMEM((n_member * members, points, LANES), F32),
+            pltpu.VMEM((n_member * members, points, LANES), F32),
+            pltpu.VMEM((n_member * flat, LANES), BF16),
             pltpu.VMEM((flat, LANES), BF16),
-            pltpu.VMEM((group, per, 32, LANES), BF16),
-            pltpu.VMEM((group, per, 32, LANES), BF16),
+            pltpu.VMEM((n_y * n_core, per, 32, LANES), BF16),
+            pltpu.VMEM((n_y * n_core, per, 32, LANES), BF16),
             pltpu.VMEM((n_z, per, 32, LANES), BF16),
             pltpu.VMEM((group, per, 32, LANES), BF16),
             pltpu.VMEM((flat, width), F32),
@@ -570,12 +651,14 @@
             pltpu.VMEM((members, points, width), F32),
             dma((6,)),
             dma((3 * width // (2 * BLOCK) + 1,)),
-            dma((2,)),
-            dma((2,)),
-            dma((n_member,)),
-            dma((n_member,)),
-            dma((group,)),
-            dma((group,)),
+            dma((HALVES, 2)),
+            dma((HALVES, 2)),
+            dma((HALVES, n_member)),
+            dma((HALVES, n_member)),
+            dma((HALVES, n_member)),
+            dma((HALVES, n_member)),
+            dma((n_y * n_core,)),
+            dma((n_y * n_core,)),
             dma((n_z,)),
             dma((n_z,)),
             dma((group,)),
@@ -587,6 +670,14 @@
             collective_id=0, has_side_effects=True, vmem_limit_bytes=VMEM_BYTES
         ),
     )(*(pltpu.with_memory_space_constraint(x, pltpu.HBM) for x in operands[:-1]), operands[-1])
+    held = [pltpu.with_memory_space_constraint(x, pltpu.VMEM) for x in (loss, grad, head)]
+    loss, grad, head = pl.pallas_call(
+        results,
+        out_shape=tuple(jax.ShapeDtypeStruct(x.shape, x.dtype) for x in held),
+        in_specs=[vmem] * 3,
+        out_specs=(hbm,) * 3,
+        scratch_shapes=[dma((3,))],
+    )(*held)
     return (loss.reshape(()), grad, head.T)
 
 

time: 50.5 us -> 45.4 us (0.90)
  Pallas kernels: 45.9 us -> 44 us
  between operations: 2.97 us -> 1.29 us
  local copies, waits for them, and re-layouts: 1.46 us -> 0 us
    pallas_call x1, Pallas kernels: 45.9 us -> 42.5 us  [body(): pl.pallas_call(functools.partial(kernel, sizes), out_shape=(jax.ShapeDtyp...]
    pallas_call x0 -> x1, Pallas kernels: none -> 1.5 us  [body(): pl.pallas_call(results, out_shape=tuple((jax.ShapeDtypeStruct(x.shape, x....]
    unnamed x2 -> x0, local copies, waits for them, and re-layouts: 1.46 us -> none
where the time goes in v3:
time: 45.4 us; the launch traced here: 45.3 us
  Pallas kernels  44 us (97%)
  between operations  1.29 us (3%)
    pallas_call x1, Pallas kernels, body(): pl.pallas_call(functools.partial(kernel, sizes), out_shape=(jax.ShapeDtyp...  42.5 us
    pallas_call x1, Pallas kernels, body(): pl.pallas_call(results, out_shape=tuple((jax.ShapeDtypeStruct(x.shape, x....  1.5 us

profile of v3, /device:TPU:1, one launch (start us, length us, event | category | flops | bytes accessed | tf_op | source)
XLA Modules:
  0.0 45.3 jit_solution(9201420670477895501)
XLA Ops:
  1.3 42.5 %shard_map.103 = (f32[1,1]{1,0:T(1,128)}, bf16[4,32,1024]{2,1,0:T(8,128)(2,1)S(1)}, f32[100,1024]{1,0:T(8,128)S(1)}) custom-call(bf16[4,32,1024]{2,1,0:T(8,128)(2,1)} %states_hbm.1, f32[1,1024]{1,0:T(1,128)} %bitcast.5, bf16[1024,3072]{1,0:T(8,128)(2,1)} %wqkv_hbm.1, bf16[1024,1024]{1,0:T(8,128)(2,1)} %wout_hbm.1, bf16[100,1024]{1,0:T(8,128)(2,1)} %bitcast.4, ...), custom_call_target="tpu_custom_call" | custom-call | tf_op jit(solution)/shard_map/pallas_call | solution.py:603
  43.8 1.5 %shard_map.104 = (f32[1,1]{1,0:T(1,128)}, bf16[4,32,1024]{2,1,0:T(8,128)(2,1)}, f32[100,1024]{1,0:T(8,128)}) custom-call(f32[1,1]{1,0:T(1,128)} %get-tuple-element.9.loss, bf16[4,32,1024]{2,1,0:T(8,128)(2,1)S(1)} %get-tuple-element.10.grad, f32[100,1024]{1,0:T(8,128)S(1)} %get-tuple-element.11.head), custom_call_target="tpu_custom_call" | custom-call | tf_op jit(solution)/shard_map/pallas_call | solution.py:674

commit v4 on v3

--- a/solution.py
+++ b/solution.py
@@ -14,7 +14,8 @@
 DELTA = 0.1
 LANES = 128
 PACK = 4
-HALVES = 2
+SPLIT = (2, 2)
+HALVES = len(SPLIT)
 VMEM_BYTES = 40 * 1024 * 1024
 BLOCK = 256
 MESH = pl.DeviceIdType.MESH
@@ -96,6 +97,8 @@
     plane_r,
     full_s,
     full_r,
+    pass_s,
+    pass_r,
     back_s,
     back_r,
 ):
@@ -146,18 +149,17 @@
     def greet(device):
         pl.semaphore_signal(barrier, inc=1, device_id=device, device_id_type=MESH)
 
-    def greet_group(k, c):
-        greet(group_peer(k))
-        return c
-
-    def greet_plane(k, c):
-        greet(plane_peer(k))
-        return c
-
-    greet((me_m, up))
-    greet((me_m, down))
-    lax.fori_loop(1, n_z, greet_plane, 0)
-    lax.fori_loop(1, group, greet_group, 0)
+    def ring(k, n):
+        return min(k, n - k)
+
+    greetings = [(0.5, (me_m, up)), (0.5, (me_m, down))]
+    greetings += [(ring(k, n_z), plane_peer(k)) for k in range(1, n_z)]
+    greetings += [
+        (ring(k // (n_y * n_core), n_member) + ring(k // n_core % n_y, n_y), group_peer(k))
+        for k in range(1, group)
+    ]
+    for _, device in sorted(greetings, key=lambda pair: -pair[0]):
+        greet(device)
 
     wide = 2 * BLOCK
     n_wide = 3 * width // wide
@@ -199,8 +201,8 @@
 
     pl.semaphore_wait(barrier, 2 + (group - 1) + (n_z - 1))
 
-    some = members // HALVES
-    band_rows = [pl.ds(h * some * points, some * points) for h in range(HALVES)]
+    firsts = [sum(SPLIT[:h]) for h in range(HALVES)]
+    band_rows = [pl.ds(first * points, some * points) for first, some in zip(firsts, SPLIT)]
     halo = [
         [
             pltpu.make_async_remote_copy(
@@ -283,11 +285,11 @@
 
     far_members = sorted(range(1, n_member), key=lambda k: -min(k, n_member - k))
     number = cnt[...]
-    for h in range(HALVES):
+    for h, (first, some) in enumerate(zip(firsts, SPLIT)):
         for copy in halo[h]:
             copy.wait_recv()
         near = beside[:, band_rows[h], :].reshape(2 * some * points, width)
-        group_members = pl.ds(h * some, some)
+        group_members = pl.ds(first, some)
         for c in range(2 * width // wide):
             here = pl.ds(c * wide, wide)
             step = dot(near, wqkv[:, pl.ds(width + c * wide, wide)], NN)
@@ -295,7 +297,7 @@
             kv[group_members, pl.ds(0, points), here] = step[0]
             kv[group_members, pl.ds(2 * points, points), here] = step[1]
 
-        pairs = [(m, p) for m in range(h * some, (h + 1) * some) for p in pack_range]
+        pairs = [(m, p) for m in range(first, first + some) for p in pack_range]
         queries = [query[pl.ds(m * points, points), heres[p]] for m, p in pairs]
         scores = [dot(kv[m, :, heres[p]], spread_heads(q), NT) for (m, p), q in zip(pairs, queries)]
         scores = [jnp.where(number > 0.0, one, -3e38) for one in scores]
@@ -427,21 +429,40 @@
             device_id_type=MESH,
         )
 
+    def area_peer(k):
+        m = lax.rem(me_m + k // n_y, n_member)
+        y = lax.rem(me_y + lax.rem(k, n_y), n_y)
+        return m, y
+
     def full_copy(k):
+        m, y = area_peer(k)
         return pltpu.make_async_remote_copy(
             src_ref=full.at[mine],
             dst_ref=full.at[mine],
             send_sem=full_s.at[k],
             recv_sem=full_r.at[k],
-            device_id=group_peer(k),
+            device_id=(m, grid_at(y, me_z, core)),
             device_id_type=MESH,
         )
 
+    def pass_copy(k):
+        m = lax.rem(me_m + n_member - k // n_y, n_member)
+        y = lax.rem(me_y + n_y - k % n_y, n_y)
+        slot = (m * n_y + y) * n_core + core
+        return pltpu.make_async_remote_copy(
+            src_ref=full.at[slot],
+            dst_ref=full.at[slot],
+            send_sem=pass_s.at[k],
+            recv_sem=pass_r.at[k],
+            device_id=(me_m, grid_at(me_y, me_z, lax.rem(core + 1, n_core))),
+            device_id_type=MESH,
+        )
+
     def apart_by(k):
-        m, y = k // (n_y * n_core), k // n_core % n_y
-        return min(m, n_member - m) + min(y, n_y - y)
-
-    far_first = sorted(range(1, group), key=lambda k: -apart_by(k))
+        return ring(k // n_y, n_member) + ring(k % n_y, n_y)
+
+    area = n_member * n_y
+    far_first = sorted(range(1, area), key=lambda k: -apart_by(k))
 
     def each(count, make, act):
         def step(k, c):
@@ -512,14 +533,18 @@
             plane_copy(k).start()
 
     for c in range(chunks):
-        if c == chunks // 2:
-            second_stage()
         here = pl.ds(c * BLOCK, BLOCK)
-        step = dot(dkv[...].reshape(members * window, 2 * width), wqkv[here, pl.ds(width, 2 * width)], NT)
+        rows = dkv[...].reshape(members * window, 2 * width)
+        step = dot(rows, wqkv[here, pl.ds(width, 2 * width)], NT)
         step = step.reshape(members, window, BLOCK)
         for side, start in ((0, 0), (1, 2 * points)):
             dsend[side, c] = step[:, start : start + points].astype(BF16)
-            back_copy(side, c).start()
+        if c == chunks // 2 - 1:
+            second_stage()
+        if c >= chunks // 2 - 1:
+            for ready in range(c + 1) if c == chunks // 2 - 1 else (c,):
+                back_copy(0, ready).start()
+                back_copy(1, ready).start()
         dhid[:, :, here] = step[:, points : 2 * points]
 
     for c in range(chunks):
@@ -534,6 +559,7 @@
     full[mine] = (split_loss(plane_sum) * (1.0 / (points * n_grid))).astype(BF16)
     for k in far_first:
         full_copy(k).start()
+    pass_copy(0).start()
     for c in range(chunks):
         here = pl.ds(c * BLOCK, BLOCK)
         for side in range(2):
@@ -549,7 +575,11 @@
         dstates = inverse[m] * (dnormed - first - norm * second)
         grad[m] = (dstates + dmixed[pl.ds(m * points, points), :]).astype(BF16)
 
-    each(group, full_copy, "wait_recv")
+    for k in reversed(far_first):
+        full_copy(k).wait_recv()
+        pass_copy(k).start()
+    for k in range(area):
+        pass_copy(k).wait_recv()
     total = jnp.zeros((1, 1), F32)
     for m in range(n_member):
         for u in range(parts * per):
@@ -569,7 +599,9 @@
             mix_copy(h, k).wait_send()
     each(parts, part_copy, "wait_send")
     each(n_z, plane_copy, "wait_send")
-    each(group, full_copy, "wait_send")
+    for k in range(area):
+        pass_copy(k).wait_send()
+    each(area, full_copy, "wait_send")
     for c in range(chunks):
         for side in range(2):
             back_copy(side, c).wait_send()
@@ -661,8 +693,10 @@
             dma((n_y * n_core,)),
             dma((n_z,)),
             dma((n_z,)),
-            dma((group,)),
-            dma((group,)),
+            dma((n_member * n_y,)),
+            dma((n_member * n_y,)),
+            dma((n_member * n_y,)),
+            dma((n_member * n_y,)),
             dma((2, chunks)),
             dma((2, chunks)),
         ],
@@ -670,11 +704,11 @@
             collective_id=0, has_side_effects=True, vmem_limit_bytes=VMEM_BYTES
         ),
     )(*(pltpu.with_memory_space_constraint(x, pltpu.HBM) for x in operands[:-1]), operands[-1])
-    held = [pltpu.with_memory_space_constraint(x, pltpu.VMEM) for x in (loss, grad, head)]
+    held = [loss, *(pltpu.with_memory_space_constraint(x, pltpu.VMEM) for x in (grad, head))]
     loss, grad, head = pl.pallas_call(
         results,
         out_shape=tuple(jax.ShapeDtypeStruct(x.shape, x.dtype) for x in held),
-        in_specs=[vmem] * 3,
+        in_specs=[hbm] * 3,
         out_specs=(hbm,) * 3,
         scratch_shapes=[dma((3,))],
     )(*held)

time: 45.4 us -> 43.6 us (0.960)
  Pallas kernels: 44 us -> 42.2 us
    pallas_call x1, Pallas kernels: 42.5 us -> 40.7 us  [body(): pl.pallas_call(functools.partial(kernel, sizes), out_shape=(jax.ShapeDtyp...]
where the time goes in v4:
time: 43.6 us; the launch traced here: 43.5 us
  Pallas kernels  42.2 us (97%)
  between operations  1.29 us (3%)
    pallas_call x1, Pallas kernels, body(): pl.pallas_call(functools.partial(kernel, sizes), out_shape=(jax.ShapeDtyp...  40.7 us
    pallas_call x1, Pallas kernels, body(): pl.pallas_call(results, out_shape=tuple((jax.ShapeDtypeStruct(x.shape, x....  1.5 us

profile of v4, /device:TPU:1, one launch (start us, length us, event | category | flops | bytes accessed | tf_op | source)
XLA Modules:
  0.0 43.5 jit_solution(7301742796380534830)
XLA Ops:
  1.3 40.7 %shard_map.103 = (f32[1,1]{1,0:T(1,128)}, bf16[4,32,1024]{2,1,0:T(8,128)(2,1)S(1)}, f32[100,1024]{1,0:T(8,128)S(1)}) custom-call(bf16[4,32,1024]{2,1,0:T(8,128)(2,1)} %states_hbm.1, f32[1,1024]{1,0:T(1,128)} %bitcast.5, bf16[1024,3072]{1,0:T(8,128)(2,1)} %wqkv_hbm.1, bf16[1024,1024]{1,0:T(8,128)(2,1)} %wout_hbm.1, bf16[100,1024]{1,0:T(8,128)(2,1)} %bitcast.4, ...), custom_call_target="tpu_custom_call" | custom-call | tf_op jit(solution)/shard_map/pallas_call | solution.py:635
  41.9 1.5 %shard_map.104 = (f32[1,1]{1,0:T(1,128)}, bf16[4,32,1024]{2,1,0:T(8,128)(2,1)}, f32[100,1024]{1,0:T(8,128)}) custom-call(f32[1,1]{1,0:T(1,128)} %get-tuple-element.9.loss, bf16[4,32,1024]{2,1,0:T(8,128)(2,1)S(1)} %get-tuple-element.10.grad, f32[100,1024]{1,0:T(8,128)S(1)} %get-tuple-element.11.head), custom_call_target="tpu_custom_call" | custom-call | tf_op jit(solution)/shard_map/pallas_call | solution.py:708

commit v5 on v4

--- a/solution.py
+++ b/solution.py
@@ -16,6 +16,7 @@
 PACK = 4
 SPLIT = (2, 2)
 HALVES = len(SPLIT)
+RELAYS = 3
 VMEM_BYTES = 40 * 1024 * 1024
 BLOCK = 256
 MESH = pl.DeviceIdType.MESH
@@ -83,6 +84,7 @@
     dsend,
     drecv,
     dhid,
+    relay,
     insem,
     wsem,
     halo_s,
@@ -144,22 +146,26 @@
     def plane_peer(k):
         return (me_m, grid_at(me_y, lax.rem(me_z + k, n_z), core))
 
-    barrier = pltpu.get_barrier_semaphore()
-
-    def greet(device):
-        pl.semaphore_signal(barrier, inc=1, device_id=device, device_id_type=MESH)
-
     def ring(k, n):
         return min(k, n - k)
 
-    greetings = [(0.5, (me_m, up)), (0.5, (me_m, down))]
-    greetings += [(ring(k, n_z), plane_peer(k)) for k in range(1, n_z)]
-    greetings += [
-        (ring(k // (n_y * n_core), n_member) + ring(k // n_core % n_y, n_y), group_peer(k))
-        for k in range(1, group)
-    ]
-    for _, device in sorted(greetings, key=lambda pair: -pair[0]):
-        greet(device)
+    def around(n):
+        return (1, n - 1) if n > 2 else (1,) * (n - 1)
+
+    neighbours_of = [(me_m, up), (me_m, down)]
+    neighbours_of += [(lax.rem(me_m + k, n_member), me_g) for k in around(n_member)]
+    neighbours_of += [(me_m, grid_at(lax.rem(me_y + k, n_y), me_z, core)) for k in around(n_y)]
+    neighbours_of += [(me_m, grid_at(me_y, lax.rem(me_z + k, n_z), core)) for k in around(n_z)]
+
+    def tell(semaphore):
+        for device in neighbours_of:
+            pl.semaphore_signal(semaphore, inc=1, device_id=device, device_id_type=MESH)
+
+    def heard(semaphore):
+        pl.semaphore_wait(semaphore, len(neighbours_of))
+
+    barrier = pltpu.get_barrier_semaphore()
+    tell(barrier)
 
     wide = 2 * BLOCK
     n_wide = 3 * width // wide
@@ -199,7 +205,7 @@
         inverse[m] = inv
         hidden[pl.ds(m * points, points), :] = (norm * gain[...]).astype(BF16)
 
-    pl.semaphore_wait(barrier, 2 + (group - 1) + (n_z - 1))
+    heard(barrier)
 
     firsts = [sum(SPLIT[:h]) for h in range(HALVES)]
     band_rows = [pl.ds(first * points, some * points) for first, some in zip(firsts, SPLIT)]
@@ -220,6 +226,7 @@
     for pair in halo:
         for copy in pair:
             copy.start()
+    tell(relay.at[0])
 
     for copy in small_copies[2:]:
         copy.wait()
@@ -249,6 +256,9 @@
         else:
             there = pl.ds(c * wide - width, wide)
             kv[:, pl.ds(points, points), there] = step.reshape(members, points, wide)
+
+    heard(relay.at[0])
+    tell(relay.at[1])
 
     def spread_heads(rows):
         return jnp.concatenate([rows] * PACK, axis=0) * hmask[...].astype(BF16)
@@ -332,6 +342,9 @@
         if h == HALVES - 1:
             for k in far_members[1:]:
                 mix_copy(h, k).start()
+        if h == 0:
+            heard(relay.at[1])
+            tell(relay.at[2])
     mix[0] = mixed[pl.ds(me_m * share, share)]
     for h in range(HALVES):
         for k in range(1, n_member):
@@ -529,6 +542,7 @@
         for k in range(1, parts):
             piece_sum = piece_sum + part[k].astype(F32)
         plane[me_z] = split_loss(piece_sum).astype(BF16)
+        heard(relay.at[2])
         for k in sorted(range(1, n_z), key=lambda k: -min(k, n_z - k)):
             plane_copy(k).start()
 
@@ -681,6 +695,7 @@
             pltpu.VMEM((2, chunks, members, points, BLOCK), BF16),
             pltpu.VMEM((2, chunks, members, points, BLOCK), BF16),
             pltpu.VMEM((members, points, width), F32),
+            pltpu.SemaphoreType.REGULAR((RELAYS,)),
             dma((6,)),
             dma((3 * width // (2 * BLOCK) + 1,)),
             dma((HALVES, 2)),

time: 43.6 us -> 43.2 us (level)
  no operation moved by 1% of the time
where the time goes in v5:
time: 43.2 us; the launch traced here: 43.1 us
  Pallas kernels  41.8 us (97%)
  between operations  1.29 us (3%)
    pallas_call x1, Pallas kernels, body(): pl.pallas_call(functools.partial(kernel, sizes), out_shape=(jax.ShapeDtyp...  40.3 us
    pallas_call x1, Pallas kernels, body(): pl.pallas_call(results, out_shape=tuple((jax.ShapeDtypeStruct(x.shape, x....  1.5 us

profile of v5, /device:TPU:1, one launch (start us, length us, event | category | flops | bytes accessed | tf_op | source)
XLA Modules:
  0.0 43.1 jit_solution(17067033969911250845)
XLA Ops:
  1.3 40.3 %shard_map.103 = (f32[1,1]{1,0:T(1,128)}, bf16[4,32,1024]{2,1,0:T(8,128)(2,1)S(1)}, f32[100,1024]{1,0:T(8,128)S(1)}) custom-call(bf16[4,32,1024]{2,1,0:T(8,128)(2,1)} %states_hbm.1, f32[1,1024]{1,0:T(1,128)} %bitcast.5, bf16[1024,3072]{1,0:T(8,128)(2,1)} %wqkv_hbm.1, bf16[1024,1024]{1,0:T(8,128)(2,1)} %wout_hbm.1, bf16[100,1024]{1,0:T(8,128)(2,1)} %bitcast.4, ...), custom_call_target="tpu_custom_call" | custom-call | tf_op jit(solution)/shard_map/pallas_call | solution.py:649
  41.6 1.5 %shard_map.104 = (f32[1,1]{1,0:T(1,128)}, bf16[4,32,1024]{2,1,0:T(8,128)(2,1)}, f32[100,1024]{1,0:T(8,128)}) custom-call(f32[1,1]{1,0:T(1,128)} %get-tuple-element.9.loss, bf16[4,32,1024]{2,1,0:T(8,128)(2,1)S(1)} %get-tuple-element.10.grad, f32[100,1024]{1,0:T(8,128)S(1)} %get-tuple-element.11.head), custom_call_target="tpu_custom_call" | custom-call | tf_op jit(solution)/shard_map/pallas_call | solution.py:723

commit v6 on v5

--- a/solution.py
+++ b/solution.py
@@ -14,8 +14,7 @@
 DELTA = 0.1
 LANES = 128
 PACK = 4
-SPLIT = (2, 2)
-HALVES = len(SPLIT)
+HALVES = 2
 RELAYS = 3
 VMEM_BYTES = 40 * 1024 * 1024
 BLOCK = 256
@@ -70,6 +69,7 @@
     ens,
     pens,
     slopes,
+    gaps,
     gradall,
     gradb,
     local,
@@ -207,25 +207,24 @@
 
     heard(barrier)
 
-    firsts = [sum(SPLIT[:h]) for h in range(HALVES)]
-    band_rows = [pl.ds(first * points, some * points) for first, some in zip(firsts, SPLIT)]
-    halo = [
-        [
-            pltpu.make_async_remote_copy(
-                src_ref=hidden.at[rows],
-                dst_ref=beside.at[i, rows],
-                send_sem=halo_s.at[h, i],
-                recv_sem=halo_r.at[h, i],
-                device_id=(me_m, side),
-                device_id_type=MESH,
-            )
-            for i, side in enumerate((up, down))
-        ]
-        for h, rows in enumerate(band_rows)
-    ]
-    for pair in halo:
-        for copy in pair:
-            copy.start()
+    some = members // HALVES
+
+    def rows_of(h):
+        return pl.ds(pl.multiple_of(h * (some * points), some * points), some * points)
+
+    def halo_copy(h, i):
+        return pltpu.make_async_remote_copy(
+            src_ref=hidden.at[rows_of(h)],
+            dst_ref=beside.at[i, rows_of(h)],
+            send_sem=halo_s.at[h, i],
+            recv_sem=halo_r.at[h, i],
+            device_id=(me_m, (up, down)[i]),
+            device_id_type=MESH,
+        )
+
+    for h in range(HALVES):
+        for i in range(2):
+            halo_copy(h, i).start()
     tell(relay.at[0])
 
     for copy in small_copies[2:]:
@@ -275,8 +274,8 @@
 
     def mix_copy(h, k):
         return pltpu.make_async_remote_copy(
-            src_ref=mixed.at[pl.ds(lax.rem(me_m + k, n_member) * share, share), band_rows[h]],
-            dst_ref=mix.at[k, :, band_rows[h]],
+            src_ref=mixed.at[pl.ds(lax.rem(me_m + k, n_member) * share, share), rows_of(h)],
+            dst_ref=mix.at[k, :, rows_of(h)],
             send_sem=mix_s.at[h, k],
             recv_sem=mix_r.at[h, k],
             device_id=(lax.rem(me_m + k, n_member), me_g),
@@ -285,8 +284,8 @@
 
     def pred_copy(h, k):
         return pltpu.make_async_remote_copy(
-            src_ref=ens.at[0, band_rows[h]],
-            dst_ref=ens.at[k, band_rows[h]],
+            src_ref=ens.at[0, rows_of(h)],
+            dst_ref=ens.at[k, rows_of(h)],
             send_sem=pred_s.at[h, k],
             recv_sem=pred_r.at[h, k],
             device_id=(lax.rem(me_m + k, n_member), me_g),
@@ -295,10 +294,12 @@
 
     far_members = sorted(range(1, n_member), key=lambda k: -min(k, n_member - k))
     number = cnt[...]
-    for h, (first, some) in enumerate(zip(firsts, SPLIT)):
-        for copy in halo[h]:
-            copy.wait_recv()
-        near = beside[:, band_rows[h], :].reshape(2 * some * points, width)
+
+    def forward(h, carry):
+        for i in range(2):
+            halo_copy(h, i).wait_recv()
+        first = h * some
+        near = beside[:, rows_of(h), :].reshape(2 * some * points, width)
         group_members = pl.ds(first, some)
         for c in range(2 * width // wide):
             here = pl.ds(c * wide, wide)
@@ -307,8 +308,10 @@
             kv[group_members, pl.ds(0, points), here] = step[0]
             kv[group_members, pl.ds(2 * points, points), here] = step[1]
 
-        pairs = [(m, p) for m in range(first, first + some) for p in pack_range]
-        queries = [query[pl.ds(m * points, points), heres[p]] for m, p in pairs]
+        pairs = [(first + m, p) for m in range(some) for p in pack_range]
+        queries = [
+            query[pl.ds(pl.multiple_of(m * points, points), points), heres[p]] for m, p in pairs
+        ]
         scores = [dot(kv[m, :, heres[p]], spread_heads(q), NT) for (m, p), q in zip(pairs, queries)]
         scores = [jnp.where(number > 0.0, one, -3e38) for one in scores]
         tops = [jnp.max(one, axis=0, keepdims=True) for one in scores]
@@ -319,11 +322,14 @@
         outs = [dot(one, kv[m, :, theres[p]], TN) for one, (m, p) in zip(weights, pairs)]
         for (m, p), one, out in zip(pairs, shares, outs):
             probs[m, p] = one
-            attn[pl.ds(m * points, points), heres[p]] = pick_heads(out).astype(BF16)
-
-        if h == 0:
+            there = pl.ds(pl.multiple_of(m * points, points), points)
+            attn[there, heres[p]] = pick_heads(out).astype(BF16)
+
+        @pl.when(h == 0)
+        def _():
             weight_copies[n_wide].wait()
-        rows = band_rows[h]
+
+        rows = rows_of(h)
         for k in (*far_members, 0):
             for c in range(share):
                 block = lax.rem(me_m + k, n_member) * share + c
@@ -331,61 +337,90 @@
                 proj = dot(attn[rows, :], wout[:, here], NN)
                 before = states[group_members, :, here].reshape(some * points, BLOCK).astype(F32)
                 mixed[block, rows] = (before + proj).astype(BF16)
-            if k != 0 and (h < HALVES - 1 or k == far_members[0]):
-                mix_copy(h, k).start()
         pred = dot(mixed[0, rows], wpad[:, pl.ds(0, BLOCK)], NT)
         for c in range(1, chunks):
             pred = pred + dot(mixed[c, rows], wpad[:, pl.ds(c * BLOCK, BLOCK)], NT)
         ens[0, rows] = pred.astype(BF16)
         for k in far_members:
             pred_copy(h, k).start()
-        if h == HALVES - 1:
-            for k in far_members[1:]:
-                mix_copy(h, k).start()
-        if h == 0:
+        for k in far_members:
+            mix_copy(h, k).start()
+
+        @pl.when(h == 0)
+        def _():
             heard(relay.at[1])
             tell(relay.at[2])
+
+        return carry
+
+    lax.fori_loop(0, HALVES, forward, 0)
     mix[0] = mixed[pl.ds(me_m * share, share)]
-    for h in range(HALVES):
-        for k in range(1, n_member):
-            pred_copy(h, k).wait_recv()
 
     step_rows = 8
-
-    def crps(block, total):
+    late = [i for i in range(held) if i >= members and i % members >= members - some]
+    early = [i for i in range(held) if i not in late]
+    everyone = [(i, j) for i in range(held) for j in range(i + 1, held)]
+    early_pairs = [(i, j) for i, j in everyone if i not in late and j not in late]
+    late_pairs = [pair for pair in everyone if pair not in early_pairs]
+
+    def widen(k, first, count):
+        rows = ens[k, pl.ds(first * points, count * points), :].astype(F32)
+        pens[pl.ds(k * members + first, count)] = rows.reshape(count, points, LANES)
+
+    def pair_sums(pairs, values, pulls, apart):
+        for i, j in pairs:
+            gap = values[i] - values[j]
+            square = gap * gap + DELTA * DELTA
+            root = lax.rsqrt(square)
+            pull = gap * root
+            pulls[i] = pull if pulls[i] is None else pulls[i] + pull
+            pulls[j] = -pull if pulls[j] is None else pulls[j] - pull
+            if i < members:
+                length = square * root
+                apart = apart + (length + length if j < members else length)
+        return apart
+
+    def crps_early(block, carry):
+        here = pl.ds(pl.multiple_of(block * step_rows, step_rows), step_rows)
+        values = {i: pens[i, here, :] for i in early}
+        pulls = [None] * held
+        gaps[here, :] = pair_sums(early_pairs, values, pulls, jnp.zeros((step_rows, LANES), F32))
+        for i in early:
+            slopes[i, here, :] = pulls[i]
+        return carry
+
+    def crps_late(block, total):
         start = pl.multiple_of(block * step_rows, step_rows)
+        here = pl.ds(start, step_rows)
         row = start + lax.broadcasted_iota(jnp.int32, (step_rows, LANES), 0)
         column = lax.broadcasted_iota(jnp.int32, (step_rows, LANES), 1)
         valid = (row < counts[0]) & (column < VARS)
-        target = tpad[pl.ds(start, step_rows), :]
-        values = [pens[i, pl.ds(start, step_rows), :] for i in range(held)]
-        pulls = [None] * held
-        apart = jnp.zeros((step_rows, LANES), F32)
-        for i in range(held):
-            for j in range(i + 1, held):
-                gap = values[i] - values[j]
-                square = gap * gap + DELTA * DELTA
-                root = lax.rsqrt(square)
-                pull = gap * root
-                pulls[i] = pull if pulls[i] is None else pulls[i] + pull
-                pulls[j] = -pull if pulls[j] is None else pulls[j] - pull
-                if i < members:
-                    length = square * root
-                    apart = apart + (length + length if j < members else length)
+        target = tpad[here, :]
+        values = [pens[i, here, :] for i in range(held)]
+        pulls = [None if i in late else slopes[i, here, :] for i in range(held)]
+        apart = pair_sums(late_pairs, values, pulls, gaps[here, :])
         terms = apart * (-0.5 / (total_members - 1))
         for i in range(held):
             miss = values[i] - target
             square = miss * miss + DELTA * DELTA
             root = lax.rsqrt(square)
             slope = miss * root - pulls[i] * (1.0 / (total_members - 1))
-            slopes[i, pl.ds(start, step_rows), :] = jnp.where(valid, slope, 0.0)
+            slopes[i, here, :] = jnp.where(valid, slope, 0.0)
             if i < members:
                 terms = terms + square * root
         return total + jnp.where(valid, terms, 0.0)
 
-    for k in range(n_member):
-        pens[pl.ds(k * members, members)] = ens[k].astype(F32).reshape(members, points, LANES)
-    terms = lax.fori_loop(0, points // step_rows, crps, jnp.zeros((step_rows, LANES), F32))
+    for h in range(HALVES - 1):
+        for k in range(1, n_member):
+            pred_copy(h, k).wait_recv()
+    widen(0, 0, members)
+    for k in range(1, n_member):
+        widen(k, 0, members - some)
+    lax.fori_loop(0, points // step_rows, crps_early, 0)
+    for k in range(1, n_member):
+        pred_copy(HALVES - 1, k).wait_recv()
+        widen(k, members - some, some)
+    terms = lax.fori_loop(0, points // step_rows, crps_late, jnp.zeros((step_rows, LANES), F32))
     loss_part = jnp.sum(jnp.sum(terms, axis=1, keepdims=True), axis=0, keepdims=True)
     gradall[...] = slopes[...].reshape(held * points, LANES).astype(BF16)
     gradb[...] = gradall[pl.ds(0, flat), :]
@@ -589,9 +624,22 @@
         dstates = inverse[m] * (dnormed - first - norm * second)
         grad[m] = (dstates + dmixed[pl.ds(m * points, points), :]).astype(BF16)
 
+    for h in range(HALVES):
+        for i in range(2):
+            halo_copy(h, i).wait_send()
+        for k in range(1, n_member):
+            pred_copy(h, k).wait_send()
+            mix_copy(h, k).wait_send()
+    each(parts, part_copy, "wait_send")
+    each(n_z, plane_copy, "wait_send")
+    for c in range(chunks):
+        for side in range(2):
+            back_copy(side, c).wait_send()
+
     for k in reversed(far_first):
         full_copy(k).wait_recv()
         pass_copy(k).start()
+    each(area, full_copy, "wait_send")
     for k in range(area):
         pass_copy(k).wait_recv()
     total = jnp.zeros((1, 1), F32)
@@ -604,21 +652,8 @@
             if u == VARS // 32:
                 total = total + tile[spot : spot + 1, 0:1] + tile[spot + 1 : spot + 2, 0:1]
     loss[...] = total * (1.0 / (VARS * total_members))
-
-    for h in range(HALVES):
-        for copy in halo[h]:
-            copy.wait_send()
-        for k in range(1, n_member):
-            pred_copy(h, k).wait_send()
-            mix_copy(h, k).wait_send()
-    each(parts, part_copy, "wait_send")
-    each(n_z, plane_copy, "wait_send")
     for k in range(area):
         pass_copy(k).wait_send()
-    each(area, full_copy, "wait_send")
-    for c in range(chunks):
-        for side in range(2):
-            back_copy(side, c).wait_send()
 
 
 def results(loss, grad, head, loss_hbm, grad_hbm, head_hbm, sem):
@@ -681,6 +716,7 @@
             pltpu.VMEM((n_member, flat, LANES), BF16),
             pltpu.VMEM((n_member * members, points, LANES), F32),
             pltpu.VMEM((n_member * members, points, LANES), F32),
+            pltpu.VMEM((points, LANES), F32),
             pltpu.VMEM((n_member * flat, LANES), BF16),
             pltpu.VMEM((flat, LANES), BF16),
             pltpu.VMEM((n_y * n_core, per, 32, LANES), BF16),

time: 43.2 us -> 42.6 us (0.986)
  Pallas kernels: 41.8 us -> 41.3 us
    pallas_call x1, Pallas kernels: 40.3 us -> 39.8 us  [body(): pl.pallas_call(functools.partial(kernel, sizes), out_shape=(jax.ShapeDtyp...]
where the time goes in v6:
time: 42.6 us; the launch traced here: 42.5 us
  Pallas kernels  41.3 us (97%)
  between operations  1.29 us (3%)
    pallas_call x1, Pallas kernels, body(): pl.pallas_call(functools.partial(kernel, sizes), out_shape=(jax.ShapeDtyp...  39.8 us
    pallas_call x1, Pallas kernels, body(): pl.pallas_call(results, out_shape=tuple((jax.ShapeDtypeStruct(x.shape, x....  1.5 us

profile of v6, /device:TPU:1, one launch (start us, length us, event | category | flops | bytes accessed | tf_op | source)
XLA Modules:
  0.0 42.5 jit_solution(16238695138944227024)
XLA Ops:
  1.3 39.8 %shard_map.103 = (f32[1,1]{1,0:T(1,128)}, bf16[4,32,1024]{2,1,0:T(8,128)(2,1)S(1)}, f32[100,1024]{1,0:T(8,128)S(1)}) custom-call(bf16[4,32,1024]{2,1,0:T(8,128)(2,1)} %states_hbm.1, f32[1,1024]{1,0:T(1,128)} %bitcast.5, bf16[1024,3072]{1,0:T(8,128)(2,1)} %wqkv_hbm.1, bf16[1024,1024]{1,0:T(8,128)(2,1)} %wout_hbm.1, bf16[100,1024]{1,0:T(8,128)(2,1)} %bitcast.4, ...), custom_call_target="tpu_custom_call" | custom-call | tf_op jit(solution)/shard_map/pallas_call | solution.py:684
  41.0 1.5 %shard_map.104 = (f32[1,1]{1,0:T(1,128)}, bf16[4,32,1024]{2,1,0:T(8,128)(2,1)}, f32[100,1024]{1,0:T(8,128)}) custom-call(f32[1,1]{1,0:T(1,128)} %get-tuple-element.9.loss, bf16[4,32,1024]{2,1,0:T(8,128)(2,1)S(1)} %get-tuple-element.10.grad, f32[100,1024]{1,0:T(8,128)S(1)} %get-tuple-element.11.head), custom_call_target="tpu_custom_call" | custom-call | tf_op jit(solution)/shard_map/pallas_call | solution.py:759

commit v7 on v6

--- a/solution.py
+++ b/solution.py
@@ -248,7 +248,9 @@
     tpad[:, pl.ds(0, VARS)] = targets[...]
 
     for c in range(n_wide):
-        weight_copies[c].wait()
+        if c % 3 == 0:
+            for d in range(c, c + 3):
+                weight_copies[d].wait()
         step = dot(hidden[...], wqkv[:, pl.ds(c * wide, wide)], NN).astype(BF16)
         if c * wide < width:
             query[:, pl.ds(c * wide, wide)] = step * jnp.asarray((width // HEADS) ** -0.5, BF16)

time: 42.6 us -> 42.4 us (level)
  no operation moved by 1% of the time
where the time goes in v7:
time: 42.4 us; the launch traced here: 42.3 us
  Pallas kernels  41 us (97%)
  between operations  1.29 us (3%)
    pallas_call x1, Pallas kernels, body(): pl.pallas_call(functools.partial(kernel, sizes), out_shape=(jax.ShapeDtyp...  39.5 us
    pallas_call x1, Pallas kernels, body(): pl.pallas_call(results, out_shape=tuple((jax.ShapeDtypeStruct(x.shape, x....  1.5 us

profile of v7, /device:TPU:1, one launch (start us, length us, event | category | flops | bytes accessed | tf_op | source)
XLA Modules:
  0.0 42.3 jit_solution(11771479331199578170)
XLA Ops:
  1.3 39.5 %shard_map.103 = (f32[1,1]{1,0:T(1,128)}, bf16[4,32,1024]{2,1,0:T(8,128)(2,1)S(1)}, f32[100,1024]{1,0:T(8,128)S(1)}) custom-call(bf16[4,32,1024]{2,1,0:T(8,128)(2,1)} %states_hbm.1, f32[1,1024]{1,0:T(1,128)} %bitcast.5, bf16[1024,3072]{1,0:T(8,128)(2,1)} %wqkv_hbm.1, bf16[1024,1024]{1,0:T(8,128)(2,1)} %wout_hbm.1, bf16[100,1024]{1,0:T(8,128)(2,1)} %bitcast.4, ...), custom_call_target="tpu_custom_call" | custom-call | tf_op jit(solution)/shard_map/pallas_call | solution.py:686
  40.8 1.5 %shard_map.104 = (f32[1,1]{1,0:T(1,128)}, bf16[4,32,1024]{2,1,0:T(8,128)(2,1)}, f32[100,1024]{1,0:T(8,128)}) custom-call(f32[1,1]{1,0:T(1,128)} %get-tuple-element.9.loss, bf16[4,32,1024]{2,1,0:T(8,128)(2,1)S(1)} %get-tuple-element.10.grad, f32[100,1024]{1,0:T(8,128)S(1)} %get-tuple-element.11.head), custom_call_target="tpu_custom_call" | custom-call | tf_op jit(solution)/shard_map/pallas_call | solution.py:761

commit v8 on v6

--- a/solution.py
+++ b/solution.py
@@ -519,7 +519,7 @@
 
         lax.fori_loop(1, count, step, 0)
 
-    for k in range(parts - 1, 0, -1):
+    for k in sorted(range(1, parts), key=lambda k: -ring(k // n_core, n_y)):
         part_copy(k).start()
 
     for c in range(chunks):

time: 42.6 us -> 42.6 us (level)
  no operation moved by 1% of the time
where the time goes in v8:
time: 42.6 us; the launch traced here: 42.5 us
  Pallas kernels  41.3 us (97%)
  between operations  1.29 us (3%)
    pallas_call x1, Pallas kernels, body(): pl.pallas_call(functools.partial(kernel, sizes), out_shape=(jax.ShapeDtyp...  39.8 us
    pallas_call x1, Pallas kernels, body(): pl.pallas_call(results, out_shape=tuple((jax.ShapeDtypeStruct(x.shape, x....  1.5 us

profile of v8, /device:TPU:1, one launch (start us, length us, event | category | flops | bytes accessed | tf_op | source)
XLA Modules:
  0.0 42.5 jit_solution(12937216550779691413)
XLA Ops:
  1.3 39.8 %shard_map.103 = (f32[1,1]{1,0:T(1,128)}, bf16[4,32,1024]{2,1,0:T(8,128)(2,1)S(1)}, f32[100,1024]{1,0:T(8,128)S(1)}) custom-call(bf16[4,32,1024]{2,1,0:T(8,128)(2,1)} %states_hbm.1, f32[1,1024]{1,0:T(1,128)} %bitcast.5, bf16[1024,3072]{1,0:T(8,128)(2,1)} %wqkv_hbm.1, bf16[1024,1024]{1,0:T(8,128)(2,1)} %wout_hbm.1, bf16[100,1024]{1,0:T(8,128)(2,1)} %bitcast.4, ...), custom_call_target="tpu_custom_call" | custom-call | tf_op jit(solution)/shard_map/pallas_call | solution.py:684
  41.0 1.5 %shard_map.104 = (f32[1,1]{1,0:T(1,128)}, bf16[4,32,1024]{2,1,0:T(8,128)(2,1)}, f32[100,1024]{1,0:T(8,128)}) custom-call(f32[1,1]{1,0:T(1,128)} %get-tuple-element.9.loss, bf16[4,32,1024]{2,1,0:T(8,128)(2,1)S(1)} %get-tuple-element.10.grad, f32[100,1024]{1,0:T(8,128)S(1)} %get-tuple-element.11.head), custom_call_target="tpu_custom_call" | custom-call | tf_op jit(solution)/shard_map/pallas_call | solution.py:759
